TPU v7x, 512 devices: a whole 4x4x16 slice. The times are simulated.
512 devices in a mesh: inj: 4 (over y), blk: 128 (over z, x, core).
Axes of the slice: x: 4, y: 4, z: 16, core: 2. Of those that a mesh axis runs over, the one named last changes fastest.
Arguments:
- tile_values: bfloat16 [1536, 128, 128], P('blk'), may hold values from -0.3125 to 0.3125
- tile_row: int32 [1536], P('blk'), may hold values from 0 to 3
- tile_dest: int32 [1536, 1], P('blk'), may hold values from 0 to 6, as said below
- trans_block: int32 [128, 21], P('blk'), may hold values from 0 to 3
- inj_pores: int32 [256, 8192], P('inj', 'blk'), may hold values from 0 to 511
- final_weight: bfloat16 [256, 65536], P('inj', 'blk'), may hold values from -6 to 6
Outputs:
- sensitivity: bfloat16 [256, 65536], P('inj', 'blk')
- tile_gradient: bfloat16 [1536, 128, 128], P('blk', 'inj')
Inputs may be any that keep to these rules, and one draw needn't show every extreme that they name: `tile_dest`: among the tiles of one index of blk, every value is named by at most 3 tiles, and 0 by exactly 3 tiles.
All inputs are finite; a program needn't handle non-finite values.
Results may differ from a plain program's by a relative error of at most 0.014.
Values may be sent and summed in bfloat16 or wider, within the bound.
A program may use at most 64 MiB of HBM per device.

v0:
```python
import jax
import jax.numpy as jnp
from jax import lax
from jax.sharding import PartitionSpec as P

NEIGH = 6
STEPS = 4


def passed_along(block, axis, distance):
    devices = range(lax.axis_size(axis))
    route = [((i - distance) % len(devices), i) for i in devices]
    return lax.ppermute(block, axis, route)


def offset_of(slot):
    amount = (slot + 1) // 2
    return amount if slot % 2 == 1 else -amount


def shards(tile_values, tile_row, tile_dest, trans_block, inj_pores, final_weight):
    tile_count = tile_values.shape[0]
    block_width = tile_values.shape[1]
    set_count = final_weight.shape[0]
    pore_count = final_weight.shape[1]
    block_count = pore_count // block_width
    send_blocks = trans_block[0]
    slot_count = send_blocks.shape[0]
    neighbours = NEIGH
    capacity = slot_count // (neighbours + 1)
    targets = tile_dest[:, 0]
    ordinal = jnp.arange(tile_count, dtype=jnp.int32)
    earlier = ordinal[:, None] > ordinal[None, :]
    position = jnp.sum(((targets[:, None] == targets[None, :]) & earlier).astype(jnp.int32), axis=1)
    slot_index = targets * capacity + position
    block_ids = jnp.arange(block_count, dtype=jnp.int32)
    row_hot = (tile_row[:, None] == block_ids[None, :]).astype(jnp.float32)
    return_hot = (send_blocks[:, None] == block_ids[None, :]).astype(jnp.bfloat16)
    set_ids = jnp.arange(set_count, dtype=jnp.int32)[:, None]
    initial = jnp.zeros((set_count, pore_count), jnp.float32).at[set_ids, inj_pores].add(1.0)
    state = initial.astype(jnp.bfloat16).reshape(set_count, block_count, block_width)

    def piece_of(buffer, slot):
        return buffer[:, slot * capacity : (slot + 1) * capacity]

    adjoint = final_weight.reshape(set_count, block_count, block_width)
    fetched = [None] * STEPS
    saved_rows = [None] * STEPS
    for timestep in range(STEPS):
        fetch_outgoing = jnp.take(state, send_blocks, axis=1)
        fetch_pieces = [piece_of(fetch_outgoing, 0)]
        for fetch_slot in range(1, neighbours + 1):
            fetch_pieces.append(
                passed_along(piece_of(fetch_outgoing, fetch_slot), "blk", -offset_of(fetch_slot))
            )
        fetch_incoming = jnp.concatenate(fetch_pieces, axis=1)
        columns = jnp.take(fetch_incoming, slot_index, axis=1)
        fetched[timestep] = columns
        if timestep + 1 < STEPS:
            contrib = jnp.einsum(
                "sib,iab->sia", columns, tile_values, preferred_element_type=jnp.float32
            )
            state = jnp.einsum(
                "sia,ic->sca", contrib, row_hot, precision=lax.Precision.HIGHEST
            ).astype(jnp.bfloat16)
    for timestep in reversed(range(STEPS)):
        adjoint_rows = jnp.take(adjoint, tile_row, axis=1)
        saved_rows[timestep] = adjoint_rows
        outgoing = (
            jnp.zeros((set_count, slot_count, block_width), jnp.bfloat16)
            .at[:, slot_index, :]
            .set(
                jnp.einsum(
                    "sia,iab->sib", adjoint_rows, tile_values, preferred_element_type=jnp.float32
                ).astype(jnp.bfloat16)
            )
        )
        send_pieces = [piece_of(outgoing, 0)]
        for send_slot in range(1, neighbours + 1):
            send_pieces.append(
                passed_along(piece_of(outgoing, send_slot), "blk", offset_of(send_slot))
            )
        incoming = jnp.concatenate(send_pieces, axis=1)
        adjoint = jnp.einsum(
            "snb,nc->scb", incoming, return_hot, preferred_element_type=jnp.float32
        ).astype(jnp.bfloat16)
    accum = jnp.zeros((tile_count, block_width, block_width), jnp.float32)
    for timestep in range(STEPS):
        accum = accum + jnp.einsum(
            "sia,sib->iab",
            saved_rows[timestep],
            fetched[timestep],
            preferred_element_type=jnp.float32,
        )
    partial_sum = accum * (1.0 / set_count)
    summed = lax.psum(partial_sum.astype(jnp.bfloat16), "inj").astype(jnp.float32)
    portion = block_width // lax.axis_size("inj")
    mine = lax.dynamic_slice_in_dim(summed, lax.axis_index("inj") * portion, portion, 1)
    return (adjoint.reshape(set_count, pore_count), mine.astype(jnp.bfloat16))


def solution(mesh):
    placed = (
        P("blk", None, None),
        P("blk"),
        P("blk", None),
        P("blk", None),
        P("inj", "blk"),
        P("inj", "blk"),
    )
    return jax.shard_map(
        shards,
        mesh=mesh,
        in_specs=placed,
        out_specs=(P("inj", "blk"), P("blk", "inj", None)),
        check_vma=False,
    )
```

profile of v0, /device:TPU:2, one launch (start us, length us, event | category | flops | bytes accessed | tf_op | source)
XLA Modules:
  0.0 321.5 jit_solution(13132654927025406320)
XLA Ops:
  11.9 1.9 collective-permute-start
  13.9 3.6 %collective-permute-start.1 = (bf16[64,3,128]{2,1,0:T(4,128)(2,1)S(1)}, bf16[64,3,128]{2,1,0:T(4,128)(2,1)S(1)}, u32[]{:S(2)}, u32[]{:S(2)}) collective-permute-start(bf16[64,3,128]{2,1,0:T(4,128)(2,1)S(1)} %copy.159), channel_id=1, source_target_pairs={{1,0},{2,1},{3,2},{4,3},{5,4},{6,5},{7,6},{8,7},{9,8},{10,9},{11,1... | collective-permute-start | bytes 147464 | tf_op jit(solution)/shard_map/ppermute | solution.py:13
  17.6 3.4 %collective-permute-start.2 = (bf16[64,3,128]{2,1,0:T(4,128)(2,1)S(1)}, bf16[64,3,128]{2,1,0:T(4,128)(2,1)S(1)}, u32[]{:S(2)}, u32[]{:S(2)}) collective-permute-start(bf16[64,3,128]{2,1,0:T(4,128)(2,1)S(1)} %copy.160), channel_id=1, source_target_pairs={{126,0},{127,1},{0,2},{1,3},{2,4},{3,5},{4,6},{5,7},{6,8},{7,9},{8... | collective-permute-start | bytes 147464 | tf_op jit(solution)/shard_map/ppermute | solution.py:13
  21.0 10.4 %collective-permute-start.3 = (bf16[64,3,128]{2,1,0:T(4,128)(2,1)S(1)}, bf16[64,3,128]{2,1,0:T(4,128)(2,1)S(1)}, u32[]{:S(2)}, u32[]{:S(2)}) collective-permute-start(bf16[64,3,128]{2,1,0:T(4,128)(2,1)S(1)} %copy.161), channel_id=1, source_target_pairs={{2,0},{3,1},{4,2},{5,3},{6,4},{7,5},{8,6},{9,7},{10,8},{11,9},{12,... | collective-permute-start | bytes 147464 | tf_op jit(solution)/shard_map/ppermute | solution.py:13
  31.5 1.9 collective-permute-start.4
  34.9 28.8 %scatter_custom_fusion.4 = f32[32768]{0:T(1024)S(1)} fusion(s32[4096]{0:T(1024)S(1)} %reshape.171, f32[4096]{0:T(1024)S(1)} %broadcast.101, f32[]{:T(128)} %constant.40.clone.1), kind=kCustom, calls=%fused_computation.80 | custom fusion | flops 4096 | bytes 131076
  64.6 7.3 %collective-permute-start.5 = (bf16[64,3,128]{2,1,0:T(4,128)(2,1)S(1)}, bf16[64,3,128]{2,1,0:T(4,128)(2,1)S(1)}, u32[]{:S(2)}, u32[]{:S(2)}) collective-permute-start(bf16[64,3,128]{2,1,0:T(4,128)(2,1)S(1)} %copy.163), channel_id=1, source_target_pairs={{3,0},{4,1},{5,2},{6,3},{7,4},{8,5},{9,6},{10,7},{11,8},{12,9},{13... | collective-permute-start | bytes 147464 | tf_op jit(solution)/shard_map/ppermute | solution.py:13
  71.9 2.0 collective-permute-start.24
  74.0 2.3 collective-permute-start.25
  76.3 7.2 %collective-permute-start.26 = (bf16[64,3,128]{2,0,1:T(8,128)(2,1)S(1)}, bf16[64,3,128]{2,0,1:T(8,128)(2,1)S(1)}, u32[]{:S(2)}, u32[]{:S(2)}) collective-permute-start(bf16[64,3,128]{2,0,1:T(8,128)(2,1)S(1)} %get-tuple-element.31), channel_id=1, source_target_pairs={{2,0},{3,1},{4,2},{5,3},{6,4},{7,5},{8,6},{9,7},{10,8},{11,9},{12,... | collective-permute-start | bytes 147464 | tf_op jit(solution)/shard_map/ppermute | solution.py:13
  83.6 1.9 collective-permute-start.27
  85.5 10.1 %collective-permute-start.28 = (bf16[64,3,128]{2,0,1:T(8,128)(2,1)S(1)}, bf16[64,3,128]{2,0,1:T(8,128)(2,1)S(1)}, u32[]{:S(2)}, u32[]{:S(2)}) collective-permute-start(bf16[64,3,128]{2,0,1:T(8,128)(2,1)S(1)} %get-tuple-element.29), channel_id=1, source_target_pairs={{3,0},{4,1},{5,2},{6,3},{7,4},{8,5},{9,6},{10,7},{11,8},{12,9},{13... | collective-permute-start | bytes 147464 | tf_op jit(solution)/shard_map/ppermute | solution.py:13
  99.3 1.9 collective-permute-start.29
  101.3 1.9 collective-permute-start.6
  103.3 3.6 %collective-permute-start.7 = (bf16[64,3,128]{2,1,0:T(4,128)(2,1)S(1)}, bf16[64,3,128]{2,1,0:T(4,128)(2,1)S(1)}, u32[]{:S(2)}, u32[]{:S(2)}) collective-permute-start(bf16[64,3,128]{2,1,0:T(4,128)(2,1)S(1)} %copy.166), channel_id=1, source_target_pairs={{1,0},{2,1},{3,2},{4,3},{5,4},{6,5},{7,6},{8,7},{9,8},{10,9},{11,1... | collective-permute-start | bytes 147464 | tf_op jit(solution)/shard_map/ppermute | solution.py:13
  107.1 1.9 collective-permute-start.8
  109.1 6.7 %collective-permute-start.9 = (bf16[64,3,128]{2,1,0:T(4,128)(2,1)S(1)}, bf16[64,3,128]{2,1,0:T(4,128)(2,1)S(1)}, u32[]{:S(2)}, u32[]{:S(2)}) collective-permute-start(bf16[64,3,128]{2,1,0:T(4,128)(2,1)S(1)} %copy.168), channel_id=1, source_target_pairs={{2,0},{3,1},{4,2},{5,3},{6,4},{7,5},{8,6},{9,7},{10,8},{11,9},{12,... | collective-permute-start | bytes 147464 | tf_op jit(solution)/shard_map/ppermute | solution.py:13
  115.8 1.9 collective-permute-start.10
  120.1 7.3 %collective-permute-start.11 = (bf16[64,3,128]{2,1,0:T(4,128)(2,1)S(1)}, bf16[64,3,128]{2,1,0:T(4,128)(2,1)S(1)}, u32[]{:S(2)}, u32[]{:S(2)}) collective-permute-start(bf16[64,3,128]{2,1,0:T(4,128)(2,1)S(1)} %copy.170), channel_id=1, source_target_pairs={{3,0},{4,1},{5,2},{6,3},{7,4},{8,5},{9,6},{10,7},{11,8},{12,9},{13... | collective-permute-start | bytes 147464 | tf_op jit(solution)/shard_map/ppermute | solution.py:13
  127.5 1.9 collective-permute-start.30
  129.4 2.4 collective-permute-start.31
  131.9 7.2 %collective-permute-start.32 = (bf16[64,3,128]{2,0,1:T(8,128)(2,1)S(1)}, bf16[64,3,128]{2,0,1:T(8,128)(2,1)S(1)}, u32[]{:S(2)}, u32[]{:S(2)}) collective-permute-start(bf16[64,3,128]{2,0,1:T(8,128)(2,1)S(1)} %get-tuple-element.24), channel_id=1, source_target_pairs={{2,0},{3,1},{4,2},{5,3},{6,4},{7,5},{8,6},{9,7},{10,8},{11,9},{12,... | collective-permute-start | bytes 147464 | tf_op jit(solution)/shard_map/ppermute | solution.py:13
  139.1 1.9 collective-permute-start.33
  141.1 10.1 %collective-permute-start.34 = (bf16[64,3,128]{2,0,1:T(8,128)(2,1)S(1)}, bf16[64,3,128]{2,0,1:T(8,128)(2,1)S(1)}, u32[]{:S(2)}, u32[]{:S(2)}) collective-permute-start(bf16[64,3,128]{2,0,1:T(8,128)(2,1)S(1)} %get-tuple-element.22), channel_id=1, source_target_pairs={{3,0},{4,1},{5,2},{6,3},{7,4},{8,5},{9,6},{10,7},{11,8},{12,9},{13... | collective-permute-start | bytes 147464 | tf_op jit(solution)/shard_map/ppermute | solution.py:13
  153.6 1.9 collective-permute-start.35
  155.7 7.0 %collective-permute-done.35 = bf16[64,3,128]{2,0,1:T(8,128)(2,1)S(1)} collective-permute-done((bf16[64,3,128]{2,0,1:T(8,128)(2,1)S(1)}, bf16[64,3,128]{2,0,1:T(8,128)(2,1)S(1)}, u32[]{:S(2)}, u32[]{:S(2)}) %collective-permute-start.35) | collective-permute-done | bytes 49184 | tf_op jit(solution)/shard_map/ppermute | solution.py:13
  165.9 1.9 collective-permute-start.12
  167.9 3.6 %collective-permute-start.13 = (bf16[64,3,128]{2,1,0:T(4,128)(2,1)S(1)}, bf16[64,3,128]{2,1,0:T(4,128)(2,1)S(1)}, u32[]{:S(2)}, u32[]{:S(2)}) collective-permute-start(bf16[64,3,128]{2,1,0:T(4,128)(2,1)S(1)} %copy.173), channel_id=1, source_target_pairs={{1,0},{2,1},{3,2},{4,3},{5,4},{6,5},{7,6},{8,7},{9,8},{10,9},{11,1... | collective-permute-start | bytes 147464 | tf_op jit(solution)/shard_map/ppermute | solution.py:13
  171.6 1.9 collective-permute-start.14
  173.6 3.9 %collective-permute-start.15 = (bf16[64,3,128]{2,1,0:T(4,128)(2,1)S(1)}, bf16[64,3,128]{2,1,0:T(4,128)(2,1)}, u32[]{:S(2)}, u32[]{:S(2)}) collective-permute-start(bf16[64,3,128]{2,1,0:T(4,128)(2,1)S(1)} %copy.175), channel_id=1, source_target_pairs={{2,0},{3,1},{4,2},{5,3},{6,4},{7,5},{8,6},{9,7},{10,8},{11,9},{12,... | collective-permute-start | bytes 147464 | tf_op jit(solution)/shard_map/ppermute | solution.py:13
  177.6 1.9 collective-permute-start.16
  181.0 7.3 %collective-permute-start.17 = (bf16[64,3,128]{2,1,0:T(4,128)(2,1)S(1)}, bf16[64,3,128]{2,1,0:T(4,128)(2,1)S(1)}, u32[]{:S(2)}, u32[]{:S(2)}) collective-permute-start(bf16[64,3,128]{2,1,0:T(4,128)(2,1)S(1)} %copy.177), channel_id=1, source_target_pairs={{3,0},{4,1},{5,2},{6,3},{7,4},{8,5},{9,6},{10,7},{11,8},{12,9},{13... | collective-permute-start | bytes 147464 | tf_op jit(solution)/shard_map/ppermute | solution.py:13
  188.4 4.4 %collective-permute-start.36 = (bf16[64,3,128]{2,0,1:T(8,128)(2,1)S(1)}, bf16[64,3,128]{2,0,1:T(8,128)(2,1)S(1)}, u32[]{:S(2)}, u32[]{:S(2)}) collective-permute-start(bf16[64,3,128]{2,0,1:T(8,128)(2,1)S(1)} %get-tuple-element.19), channel_id=1, source_target_pairs={{1,0},{2,1},{3,2},{4,3},{5,4},{6,5},{7,6},{8,7},{9,8},{10,9},{11,1... | collective-permute-start | bytes 147464 | tf_op jit(solution)/shard_map/ppermute | solution.py:13
  194.7 4.3 %collective-permute-start.38 = (bf16[64,3,128]{2,0,1:T(8,128)(2,1)S(1)}, bf16[64,3,128]{2,0,1:T(8,128)(2,1)S(1)}, u32[]{:S(2)}, u32[]{:S(2)}) collective-permute-start(bf16[64,3,128]{2,0,1:T(8,128)(2,1)S(1)} %get-tuple-element.17), channel_id=1, source_target_pairs={{2,0},{3,1},{4,2},{5,3},{6,4},{7,5},{8,6},{9,7},{10,8},{11,9},{12,... | collective-permute-start | bytes 147464 | tf_op jit(solution)/shard_map/ppermute | solution.py:13
  201.0 10.1 %collective-permute-start.40 = (bf16[64,3,128]{2,0,1:T(8,128)(2,1)S(1)}, bf16[64,3,128]{2,0,1:T(8,128)(2,1)S(1)}, u32[]{:S(2)}, u32[]{:S(2)}) collective-permute-start(bf16[64,3,128]{2,0,1:T(8,128)(2,1)S(1)} %get-tuple-element.15), channel_id=1, source_target_pairs={{3,0},{4,1},{5,2},{6,3},{7,4},{8,5},{9,6},{10,7},{11,8},{12,9},{13... | collective-permute-start | bytes 147464 | tf_op jit(solution)/shard_map/ppermute | solution.py:13
  211.1 3.6 %concatenate.29 = bf16[64,21,128]{2,1,0:T(8,128)(2,1)S(1)} concatenate(bf16[64,3,128]{2,1,0:T(4,128)(2,1)S(1)} %copy.171, bf16[64,3,128]{2,1,0:T(4,128)(2,1)S(1)} %collective-permute-done.12, bf16[64,3,128]{2,1,0:T(4,128)(2,1)S(1)} %collective-permute-done.13, bf16[64,3,128]{2,1,0:T(4,128)(2,1)} %collective-permute-done.14, bf16[64,3,128]{2,1,0:T(4,128)(2,1)} %collective-permute-done.15, ...), dimensions={1} | concatenate | bytes 688128 | tf_op jit(solution)/shard_map/concatenate | solution.py:83
  214.9 2.1 collective-permute-start.41
  217.7 6.2 %collective-permute-done.41 = bf16[64,3,128]{2,0,1:T(8,128)(2,1)S(1)} collective-permute-done((bf16[64,3,128]{2,0,1:T(8,128)(2,1)S(1)}, bf16[64,3,128]{2,0,1:T(8,128)(2,1)S(1)}, u32[]{:S(2)}, u32[]{:S(2)}) %collective-permute-start.41) | collective-permute-done | bytes 49184 | tf_op jit(solution)/shard_map/ppermute | solution.py:13
  229.4 2.4 collective-permute-start.43
  231.8 2.0 collective-permute-start.44
  233.8 3.9 %collective-permute-start.45 = (bf16[64,3,128]{2,0,1:T(8,128)(2,1)S(1)}, bf16[64,3,128]{2,0,1:T(8,128)(2,1)S(1)}, u32[]{:S(2)}, u32[]{:S(2)}) collective-permute-start(bf16[64,3,128]{2,0,1:T(8,128)(2,1)S(1)} %get-tuple-element.9), channel_id=1, source_target_pairs={{126,0},{127,1},{0,2},{1,3},{2,4},{3,5},{4,6},{5,7},{6,8},{7,9},{8... | collective-permute-start | bytes 147464 | tf_op jit(solution)/shard_map/ppermute | solution.py:13
  237.7 8.6 %collective-permute-start.46 = (bf16[64,3,128]{2,0,1:T(8,128)(2,1)S(1)}, bf16[64,3,128]{2,0,1:T(8,128)(2,1)S(1)}, u32[]{:S(2)}, u32[]{:S(2)}) collective-permute-start(bf16[64,3,128]{2,0,1:T(8,128)(2,1)S(1)} %get-tuple-element.8), channel_id=1, source_target_pairs={{3,0},{4,1},{5,2},{6,3},{7,4},{8,5},{9,6},{10,7},{11,8},{12,9},{13... | collective-permute-start | bytes 147464 | tf_op jit(solution)/shard_map/ppermute | solution.py:13
  249.6 7.0 %collective-permute-done.47 = bf16[64,3,128]{2,0,1:T(8,128)(2,1)S(1)} collective-permute-done((bf16[64,3,128]{2,0,1:T(8,128)(2,1)S(1)}, bf16[64,3,128]{2,0,1:T(8,128)(2,1)S(1)}, u32[]{:S(2)}, u32[]{:S(2)}) %collective-permute-start.47) | collective-permute-done | bytes 49184 | tf_op jit(solution)/shard_map/ppermute | solution.py:13
  258.5 1.9 collective-permute-start.18
  260.5 3.6 %collective-permute-start.19 = (bf16[64,3,128]{2,1,0:T(4,128)(2,1)S(1)}, bf16[64,3,128]{2,1,0:T(4,128)(2,1)S(1)}, u32[]{:S(2)}, u32[]{:S(2)}) collective-permute-start(bf16[64,3,128]{2,1,0:T(4,128)(2,1)S(1)} %copy.180), channel_id=1, source_target_pairs={{1,0},{2,1},{3,2},{4,3},{5,4},{6,5},{7,6},{8,7},{9,8},{10,9},{11,1... | collective-permute-start | bytes 147464 | tf_op jit(solution)/shard_map/ppermute | solution.py:13
  266.2 3.9 %collective-permute-start.21 = (bf16[64,3,128]{2,1,0:T(4,128)(2,1)S(1)}, bf16[64,3,128]{2,1,0:T(4,128)(2,1)S(1)}, u32[]{:S(2)}, u32[]{:S(2)}) collective-permute-start(bf16[64,3,128]{2,1,0:T(4,128)(2,1)S(1)} %copy.182), channel_id=1, source_target_pairs={{2,0},{3,1},{4,2},{5,3},{6,4},{7,5},{8,6},{9,7},{10,8},{11,9},{12,... | collective-permute-start | bytes 147464 | tf_op jit(solution)/shard_map/ppermute | solution.py:13
  272.1 7.3 %collective-permute-start.23 = (bf16[64,3,128]{2,1,0:T(4,128)(2,1)S(1)}, bf16[64,3,128]{2,1,0:T(4,128)(2,1)S(1)}, u32[]{:S(2)}, u32[]{:S(2)}) collective-permute-start(bf16[64,3,128]{2,1,0:T(4,128)(2,1)S(1)} %copy.184), channel_id=1, source_target_pairs={{3,0},{4,1},{5,2},{6,3},{7,4},{8,5},{9,6},{10,7},{11,8},{12,9},{13... | collective-permute-start | bytes 147464 | tf_op jit(solution)/shard_map/ppermute | solution.py:13
  283.5 29.6 %all-reduce.2.cloned.1.call-done = bf16[12,128,128]{2,1,0:T(8,128)(2,1)} async-done(((bf16[12,128,128]{2,1,0:T(8,128)(2,1)}), bf16[12,128,128]{2,1,0:T(8,128)(2,1)}) %all-reduce.2.cloned.1.call-update) | async-done | bytes 393232 | tf_op jit(solution)/shard_map/psum | solution.py:96
  (216 shorter events, 45.7 us)
Async XLA Ops:
  7.2 305.9 %all-reduce.2.cloned.1.call-start = ((), (), s32[]{:S(2)}) async-start(), calls=%async_computation | async-start | bytes 786432 | tf_op jit(solution)/shard_map/psum | solution.py:96
  11.9 52.7 %collective-permute-start = (bf16[64,3,128]{2,1,0:T(4,128)(2,1)S(1)}, bf16[64,3,128]{2,1,0:T(4,128)(2,1)S(1)}, u32[]{:S(2)}, u32[]{:S(2)}) collective-permute-start(bf16[64,3,128]{2,1,0:T(4,128)(2,1)S(1)} %copy.158), channel_id=1, source_target_pairs={{127,0},{0,1},{1,2},{2,3},{3,4},{4,5},{5,6},{6,7},{7,8},{8,9},{9,1... | collective-permute-start | bytes 147464 | tf_op jit(solution)/shard_map/ppermute | solution.py:13
  13.9 58.1 %collective-permute-start.1 = (bf16[64,3,128]{2,1,0:T(4,128)(2,1)S(1)}, bf16[64,3,128]{2,1,0:T(4,128)(2,1)S(1)}, u32[]{:S(2)}, u32[]{:S(2)}) collective-permute-start(bf16[64,3,128]{2,1,0:T(4,128)(2,1)S(1)} %copy.159), channel_id=1, source_target_pairs={{1,0},{2,1},{3,2},{4,3},{5,4},{6,5},{7,6},{8,7},{9,8},{10,9},{11,1... | collective-permute-start | bytes 147464 | tf_op jit(solution)/shard_map/ppermute | solution.py:13
  17.6 56.4 %collective-permute-start.2 = (bf16[64,3,128]{2,1,0:T(4,128)(2,1)S(1)}, bf16[64,3,128]{2,1,0:T(4,128)(2,1)S(1)}, u32[]{:S(2)}, u32[]{:S(2)}) collective-permute-start(bf16[64,3,128]{2,1,0:T(4,128)(2,1)S(1)} %copy.160), channel_id=1, source_target_pairs={{126,0},{127,1},{0,2},{1,3},{2,4},{3,5},{4,6},{5,7},{6,8},{7,9},{8... | collective-permute-start | bytes 147464 | tf_op jit(solution)/shard_map/ppermute | solution.py:13
  21.0 55.3 %collective-permute-start.3 = (bf16[64,3,128]{2,1,0:T(4,128)(2,1)S(1)}, bf16[64,3,128]{2,1,0:T(4,128)(2,1)S(1)}, u32[]{:S(2)}, u32[]{:S(2)}) collective-permute-start(bf16[64,3,128]{2,1,0:T(4,128)(2,1)S(1)} %copy.161), channel_id=1, source_target_pairs={{2,0},{3,1},{4,2},{5,3},{6,4},{7,5},{8,6},{9,7},{10,8},{11,9},{12,... | collective-permute-start | bytes 147464 | tf_op jit(solution)/shard_map/ppermute | solution.py:13
  31.5 52.1 %collective-permute-start.4 = (bf16[64,3,128]{2,1,0:T(4,128)(2,1)S(1)}, bf16[64,3,128]{2,1,0:T(4,128)(2,1)S(1)}, u32[]{:S(2)}, u32[]{:S(2)}) collective-permute-start(bf16[64,3,128]{2,1,0:T(4,128)(2,1)S(1)} %copy.162), channel_id=1, source_target_pairs={{125,0},{126,1},{127,2},{0,3},{1,4},{2,5},{3,6},{4,7},{5,8},{6,9},... | collective-permute-start | bytes 147464 | tf_op jit(solution)/shard_map/ppermute | solution.py:13
  64.6 20.9 %collective-permute-start.5 = (bf16[64,3,128]{2,1,0:T(4,128)(2,1)S(1)}, bf16[64,3,128]{2,1,0:T(4,128)(2,1)S(1)}, u32[]{:S(2)}, u32[]{:S(2)}) collective-permute-start(bf16[64,3,128]{2,1,0:T(4,128)(2,1)S(1)} %copy.163), channel_id=1, source_target_pairs={{3,0},{4,1},{5,2},{6,3},{7,4},{8,5},{9,6},{10,7},{11,8},{12,9},{13... | collective-permute-start | bytes 147464 | tf_op jit(solution)/shard_map/ppermute | solution.py:13
  71.9 27.3 %collective-permute-start.24 = (bf16[64,3,128]{2,0,1:T(8,128)(2,1)S(1)}, bf16[64,3,128]{2,0,1:T(8,128)(2,1)S(1)}, u32[]{:S(2)}, u32[]{:S(2)}) collective-permute-start(bf16[64,3,128]{2,0,1:T(8,128)(2,1)S(1)} %get-tuple-element.33), channel_id=1, source_target_pairs={{1,0},{2,1},{3,2},{4,3},{5,4},{6,5},{7,6},{8,7},{9,8},{10,9},{11,1... | collective-permute-start | bytes 147464 | tf_op jit(solution)/shard_map/ppermute | solution.py:13
  74.0 27.3 %collective-permute-start.25 = (bf16[64,3,128]{2,0,1:T(8,128)(2,1)S(1)}, bf16[64,3,128]{2,0,1:T(8,128)(2,1)S(1)}, u32[]{:S(2)}, u32[]{:S(2)}) collective-permute-start(bf16[64,3,128]{2,0,1:T(8,128)(2,1)S(1)} %get-tuple-element.32), channel_id=1, source_target_pairs={{127,0},{0,1},{1,2},{2,3},{3,4},{4,5},{5,6},{6,7},{7,8},{8,9},{9,1... | collective-permute-start | bytes 147464 | tf_op jit(solution)/shard_map/ppermute | solution.py:13
  76.3 27.0 %collective-permute-start.26 = (bf16[64,3,128]{2,0,1:T(8,128)(2,1)S(1)}, bf16[64,3,128]{2,0,1:T(8,128)(2,1)S(1)}, u32[]{:S(2)}, u32[]{:S(2)}) collective-permute-start(bf16[64,3,128]{2,0,1:T(8,128)(2,1)S(1)} %get-tuple-element.31), channel_id=1, source_target_pairs={{2,0},{3,1},{4,2},{5,3},{6,4},{7,5},{8,6},{9,7},{10,8},{11,9},{12,... | collective-permute-start | bytes 147464 | tf_op jit(solution)/shard_map/ppermute | solution.py:13
  83.6 23.5 %collective-permute-start.27 = (bf16[64,3,128]{2,0,1:T(8,128)(2,1)S(1)}, bf16[64,3,128]{2,0,1:T(8,128)(2,1)S(1)}, u32[]{:S(2)}, u32[]{:S(2)}) collective-permute-start(bf16[64,3,128]{2,0,1:T(8,128)(2,1)S(1)} %get-tuple-element.30), channel_id=1, source_target_pairs={{126,0},{127,1},{0,2},{1,3},{2,4},{3,5},{4,6},{5,7},{6,8},{7,9},{8... | collective-permute-start | bytes 147464 | tf_op jit(solution)/shard_map/ppermute | solution.py:13
  85.5 23.5 %collective-permute-start.28 = (bf16[64,3,128]{2,0,1:T(8,128)(2,1)S(1)}, bf16[64,3,128]{2,0,1:T(8,128)(2,1)S(1)}, u32[]{:S(2)}, u32[]{:S(2)}) collective-permute-start(bf16[64,3,128]{2,0,1:T(8,128)(2,1)S(1)} %get-tuple-element.29), channel_id=1, source_target_pairs={{3,0},{4,1},{5,2},{6,3},{7,4},{8,5},{9,6},{10,7},{11,8},{12,9},{13... | collective-permute-start | bytes 147464 | tf_op jit(solution)/shard_map/ppermute | solution.py:13
  99.3 16.5 %collective-permute-start.29 = (bf16[64,3,128]{2,0,1:T(8,128)(2,1)S(1)}, bf16[64,3,128]{2,0,1:T(8,128)(2,1)S(1)}, u32[]{:S(2)}, u32[]{:S(2)}) collective-permute-start(bf16[64,3,128]{2,0,1:T(8,128)(2,1)S(1)} %get-tuple-element.28), channel_id=1, source_target_pairs={{125,0},{126,1},{127,2},{0,3},{1,4},{2,5},{3,6},{4,7},{5,8},{6,9},... | collective-permute-start | bytes 147464 | tf_op jit(solution)/shard_map/ppermute | solution.py:13
  101.3 18.8 %collective-permute-start.6 = (bf16[64,3,128]{2,1,0:T(4,128)(2,1)S(1)}, bf16[64,3,128]{2,1,0:T(4,128)(2,1)S(1)}, u32[]{:S(2)}, u32[]{:S(2)}) collective-permute-start(bf16[64,3,128]{2,1,0:T(4,128)(2,1)S(1)} %copy.165), channel_id=1, source_target_pairs={{127,0},{0,1},{1,2},{2,3},{3,4},{4,5},{5,6},{6,7},{7,8},{8,9},{9,1... | collective-permute-start | bytes 147464 | tf_op jit(solution)/shard_map/ppermute | solution.py:13
  103.3 24.2 %collective-permute-start.7 = (bf16[64,3,128]{2,1,0:T(4,128)(2,1)S(1)}, bf16[64,3,128]{2,1,0:T(4,128)(2,1)S(1)}, u32[]{:S(2)}, u32[]{:S(2)}) collective-permute-start(bf16[64,3,128]{2,1,0:T(4,128)(2,1)S(1)} %copy.166), channel_id=1, source_target_pairs={{1,0},{2,1},{3,2},{4,3},{5,4},{6,5},{7,6},{8,7},{9,8},{10,9},{11,1... | collective-permute-start | bytes 147464 | tf_op jit(solution)/shard_map/ppermute | solution.py:13
  107.1 22.4 %collective-permute-start.8 = (bf16[64,3,128]{2,1,0:T(4,128)(2,1)S(1)}, bf16[64,3,128]{2,1,0:T(4,128)(2,1)S(1)}, u32[]{:S(2)}, u32[]{:S(2)}) collective-permute-start(bf16[64,3,128]{2,1,0:T(4,128)(2,1)S(1)} %copy.167), channel_id=1, source_target_pairs={{126,0},{127,1},{0,2},{1,3},{2,4},{3,5},{4,6},{5,7},{6,8},{7,9},{8... | collective-permute-start | bytes 147464 | tf_op jit(solution)/shard_map/ppermute | solution.py:13
  109.1 22.8 %collective-permute-start.9 = (bf16[64,3,128]{2,1,0:T(4,128)(2,1)S(1)}, bf16[64,3,128]{2,1,0:T(4,128)(2,1)S(1)}, u32[]{:S(2)}, u32[]{:S(2)}) collective-permute-start(bf16[64,3,128]{2,1,0:T(4,128)(2,1)S(1)} %copy.168), channel_id=1, source_target_pairs={{2,0},{3,1},{4,2},{5,3},{6,4},{7,5},{8,6},{9,7},{10,8},{11,9},{12,... | collective-permute-start | bytes 147464 | tf_op jit(solution)/shard_map/ppermute | solution.py:13
  115.8 23.3 %collective-permute-start.10 = (bf16[64,3,128]{2,1,0:T(4,128)(2,1)S(1)}, bf16[64,3,128]{2,1,0:T(4,128)(2,1)S(1)}, u32[]{:S(2)}, u32[]{:S(2)}) collective-permute-start(bf16[64,3,128]{2,1,0:T(4,128)(2,1)S(1)} %copy.169), channel_id=1, source_target_pairs={{125,0},{126,1},{127,2},{0,3},{1,4},{2,5},{3,6},{4,7},{5,8},{6,9},... | collective-permute-start | bytes 147464 | tf_op jit(solution)/shard_map/ppermute | solution.py:13
  120.1 20.9 %collective-permute-start.11 = (bf16[64,3,128]{2,1,0:T(4,128)(2,1)S(1)}, bf16[64,3,128]{2,1,0:T(4,128)(2,1)S(1)}, u32[]{:S(2)}, u32[]{:S(2)}) collective-permute-start(bf16[64,3,128]{2,1,0:T(4,128)(2,1)S(1)} %copy.170), channel_id=1, source_target_pairs={{3,0},{4,1},{5,2},{6,3},{7,4},{8,5},{9,6},{10,7},{11,8},{12,9},{13... | collective-permute-start | bytes 147464 | tf_op jit(solution)/shard_map/ppermute | solution.py:13
  127.5 26.1 %collective-permute-start.30 = (bf16[64,3,128]{2,0,1:T(8,128)(2,1)S(1)}, bf16[64,3,128]{2,0,1:T(8,128)(2,1)S(1)}, u32[]{:S(2)}, u32[]{:S(2)}) collective-permute-start(bf16[64,3,128]{2,0,1:T(8,128)(2,1)S(1)} %get-tuple-element.26), channel_id=1, source_target_pairs={{1,0},{2,1},{3,2},{4,3},{5,4},{6,5},{7,6},{8,7},{9,8},{10,9},{11,1... | collective-permute-start | bytes 147464 | tf_op jit(solution)/shard_map/ppermute | solution.py:13
  129.4 26.1 %collective-permute-start.31 = (bf16[64,3,128]{2,0,1:T(8,128)(2,1)S(1)}, bf16[64,3,128]{2,0,1:T(8,128)(2,1)S(1)}, u32[]{:S(2)}, u32[]{:S(2)}) collective-permute-start(bf16[64,3,128]{2,0,1:T(8,128)(2,1)S(1)} %get-tuple-element.25), channel_id=1, source_target_pairs={{127,0},{0,1},{1,2},{2,3},{3,4},{4,5},{5,6},{6,7},{7,8},{8,9},{9,1... | collective-permute-start | bytes 147464 | tf_op jit(solution)/shard_map/ppermute | solution.py:13
  131.9 23.7 %collective-permute-start.32 = (bf16[64,3,128]{2,0,1:T(8,128)(2,1)S(1)}, bf16[64,3,128]{2,0,1:T(8,128)(2,1)S(1)}, u32[]{:S(2)}, u32[]{:S(2)}) collective-permute-start(bf16[64,3,128]{2,0,1:T(8,128)(2,1)S(1)} %get-tuple-element.24), channel_id=1, source_target_pairs={{2,0},{3,1},{4,2},{5,3},{6,4},{7,5},{8,6},{9,7},{10,8},{11,9},{12,... | collective-permute-start | bytes 147464 | tf_op jit(solution)/shard_map/ppermute | solution.py:13
  139.1 16.5 %collective-permute-start.33 = (bf16[64,3,128]{2,0,1:T(8,128)(2,1)S(1)}, bf16[64,3,128]{2,0,1:T(8,128)(2,1)S(1)}, u32[]{:S(2)}, u32[]{:S(2)}) collective-permute-start(bf16[64,3,128]{2,0,1:T(8,128)(2,1)S(1)} %get-tuple-element.23), channel_id=1, source_target_pairs={{126,0},{127,1},{0,2},{1,3},{2,4},{3,5},{4,6},{5,7},{6,8},{7,9},{8... | collective-permute-start | bytes 147464 | tf_op jit(solution)/shard_map/ppermute | solution.py:13
  141.1 14.6 %collective-permute-start.34 = (bf16[64,3,128]{2,0,1:T(8,128)(2,1)S(1)}, bf16[64,3,128]{2,0,1:T(8,128)(2,1)S(1)}, u32[]{:S(2)}, u32[]{:S(2)}) collective-permute-start(bf16[64,3,128]{2,0,1:T(8,128)(2,1)S(1)} %get-tuple-element.22), channel_id=1, source_target_pairs={{3,0},{4,1},{5,2},{6,3},{7,4},{8,5},{9,6},{10,7},{11,8},{12,9},{13... | collective-permute-start | bytes 147464 | tf_op jit(solution)/shard_map/ppermute | solution.py:13
  153.6 9.0 %collective-permute-start.35 = (bf16[64,3,128]{2,0,1:T(8,128)(2,1)S(1)}, bf16[64,3,128]{2,0,1:T(8,128)(2,1)S(1)}, u32[]{:S(2)}, u32[]{:S(2)}) collective-permute-start(bf16[64,3,128]{2,0,1:T(8,128)(2,1)S(1)} %get-tuple-element.21), channel_id=1, source_target_pairs={{125,0},{126,1},{127,2},{0,3},{1,4},{2,5},{3,6},{4,7},{5,8},{6,9},... | collective-permute-start | bytes 147464 | tf_op jit(solution)/shard_map/ppermute | solution.py:13
  165.9 15.1 %collective-permute-start.12 = (bf16[64,3,128]{2,1,0:T(4,128)(2,1)S(1)}, bf16[64,3,128]{2,1,0:T(4,128)(2,1)S(1)}, u32[]{:S(2)}, u32[]{:S(2)}) collective-permute-start(bf16[64,3,128]{2,1,0:T(4,128)(2,1)S(1)} %copy.172), channel_id=1, source_target_pairs={{127,0},{0,1},{1,2},{2,3},{3,4},{4,5},{5,6},{6,7},{7,8},{8,9},{9,1... | collective-permute-start | bytes 147464 | tf_op jit(solution)/shard_map/ppermute | solution.py:13
  167.9 20.4 %collective-permute-start.13 = (bf16[64,3,128]{2,1,0:T(4,128)(2,1)S(1)}, bf16[64,3,128]{2,1,0:T(4,128)(2,1)S(1)}, u32[]{:S(2)}, u32[]{:S(2)}) collective-permute-start(bf16[64,3,128]{2,1,0:T(4,128)(2,1)S(1)} %copy.173), channel_id=1, source_target_pairs={{1,0},{2,1},{3,2},{4,3},{5,4},{6,5},{7,6},{8,7},{9,8},{10,9},{11,1... | collective-permute-start | bytes 147464 | tf_op jit(solution)/shard_map/ppermute | solution.py:13
  171.6 21.2 %collective-permute-start.14 = (bf16[64,3,128]{2,1,0:T(4,128)(2,1)S(1)}, bf16[64,3,128]{2,1,0:T(4,128)(2,1)}, u32[]{:S(2)}, u32[]{:S(2)}) collective-permute-start(bf16[64,3,128]{2,1,0:T(4,128)(2,1)S(1)} %copy.174), channel_id=1, source_target_pairs={{126,0},{127,1},{0,2},{1,3},{2,4},{3,5},{4,6},{5,7},{6,8},{7,9},{8... | collective-permute-start | bytes 147464 | tf_op jit(solution)/shard_map/ppermute | solution.py:13
  173.6 21.1 %collective-permute-start.15 = (bf16[64,3,128]{2,1,0:T(4,128)(2,1)S(1)}, bf16[64,3,128]{2,1,0:T(4,128)(2,1)}, u32[]{:S(2)}, u32[]{:S(2)}) collective-permute-start(bf16[64,3,128]{2,1,0:T(4,128)(2,1)S(1)} %copy.175), channel_id=1, source_target_pairs={{2,0},{3,1},{4,2},{5,3},{6,4},{7,5},{8,6},{9,7},{10,8},{11,9},{12,... | collective-permute-start | bytes 147464 | tf_op jit(solution)/shard_map/ppermute | solution.py:13
  177.6 21.5 %collective-permute-start.16 = (bf16[64,3,128]{2,1,0:T(4,128)(2,1)S(1)}, bf16[64,3,128]{2,1,0:T(4,128)(2,1)}, u32[]{:S(2)}, u32[]{:S(2)}) collective-permute-start(bf16[64,3,128]{2,1,0:T(4,128)(2,1)S(1)} %copy.176), channel_id=1, source_target_pairs={{125,0},{126,1},{127,2},{0,3},{1,4},{2,5},{3,6},{4,7},{5,8},{6,9},... | collective-permute-start | bytes 147464 | tf_op jit(solution)/shard_map/ppermute | solution.py:13
  181.0 20.0 %collective-permute-start.17 = (bf16[64,3,128]{2,1,0:T(4,128)(2,1)S(1)}, bf16[64,3,128]{2,1,0:T(4,128)(2,1)S(1)}, u32[]{:S(2)}, u32[]{:S(2)}) collective-permute-start(bf16[64,3,128]{2,1,0:T(4,128)(2,1)S(1)} %copy.177), channel_id=1, source_target_pairs={{3,0},{4,1},{5,2},{6,3},{7,4},{8,5},{9,6},{10,7},{11,8},{12,9},{13... | collective-permute-start | bytes 147464 | tf_op jit(solution)/shard_map/ppermute | solution.py:13
  188.4 26.5 %collective-permute-start.36 = (bf16[64,3,128]{2,0,1:T(8,128)(2,1)S(1)}, bf16[64,3,128]{2,0,1:T(8,128)(2,1)S(1)}, u32[]{:S(2)}, u32[]{:S(2)}) collective-permute-start(bf16[64,3,128]{2,0,1:T(8,128)(2,1)S(1)} %get-tuple-element.19), channel_id=1, source_target_pairs={{1,0},{2,1},{3,2},{4,3},{5,4},{6,5},{7,6},{8,7},{9,8},{10,9},{11,1... | collective-permute-start | bytes 147464 | tf_op jit(solution)/shard_map/ppermute | solution.py:13
  192.8 24.2 %collective-permute-start.37 = (bf16[64,3,128]{2,0,1:T(8,128)(2,1)S(1)}, bf16[64,3,128]{2,0,1:T(8,128)(2,1)S(1)}, u32[]{:S(2)}, u32[]{:S(2)}) collective-permute-start(bf16[64,3,128]{2,0,1:T(8,128)(2,1)S(1)} %get-tuple-element.18), channel_id=1, source_target_pairs={{127,0},{0,1},{1,2},{2,3},{3,4},{4,5},{5,6},{6,7},{7,8},{8,9},{9,1... | collective-permute-start | bytes 147464 | tf_op jit(solution)/shard_map/ppermute | solution.py:13
  194.7 22.3 %collective-permute-start.38 = (bf16[64,3,128]{2,0,1:T(8,128)(2,1)S(1)}, bf16[64,3,128]{2,0,1:T(8,128)(2,1)S(1)}, u32[]{:S(2)}, u32[]{:S(2)}) collective-permute-start(bf16[64,3,128]{2,0,1:T(8,128)(2,1)S(1)} %get-tuple-element.17), channel_id=1, source_target_pairs={{2,0},{3,1},{4,2},{5,3},{6,4},{7,5},{8,6},{9,7},{10,8},{11,9},{12,... | collective-permute-start | bytes 147464 | tf_op jit(solution)/shard_map/ppermute | solution.py:13
  199.1 18.0 %collective-permute-start.39 = (bf16[64,3,128]{2,0,1:T(8,128)(2,1)S(1)}, bf16[64,3,128]{2,0,1:T(8,128)(2,1)S(1)}, u32[]{:S(2)}, u32[]{:S(2)}) collective-permute-start(bf16[64,3,128]{2,0,1:T(8,128)(2,1)S(1)} %get-tuple-element.16), channel_id=1, source_target_pairs={{126,0},{127,1},{0,2},{1,3},{2,4},{3,5},{4,6},{5,7},{6,8},{7,9},{8... | collective-permute-start | bytes 147464 | tf_op jit(solution)/shard_map/ppermute | solution.py:13
  201.0 16.1 %collective-permute-start.40 = (bf16[64,3,128]{2,0,1:T(8,128)(2,1)S(1)}, bf16[64,3,128]{2,0,1:T(8,128)(2,1)S(1)}, u32[]{:S(2)}, u32[]{:S(2)}) collective-permute-start(bf16[64,3,128]{2,0,1:T(8,128)(2,1)S(1)} %get-tuple-element.15), channel_id=1, source_target_pairs={{3,0},{4,1},{5,2},{6,3},{7,4},{8,5},{9,6},{10,7},{11,8},{12,9},{13... | collective-permute-start | bytes 147464 | tf_op jit(solution)/shard_map/ppermute | solution.py:13
  227.2 20.4 %collective-permute-start.42 = (bf16[64,3,128]{2,0,1:T(8,128)(2,1)S(1)}, bf16[64,3,128]{2,0,1:T(8,128)(2,1)S(1)}, u32[]{:S(2)}, u32[]{:S(2)}) collective-permute-start(bf16[64,3,128]{2,0,1:T(8,128)(2,1)S(1)} %get-tuple-element.12), channel_id=1, source_target_pairs={{1,0},{2,1},{3,2},{4,3},{5,4},{6,5},{7,6},{8,7},{9,8},{10,9},{11,1... | collective-permute-start | bytes 147464 | tf_op jit(solution)/shard_map/ppermute | solution.py:13
  229.4 20.1 %collective-permute-start.43 = (bf16[64,3,128]{2,0,1:T(8,128)(2,1)S(1)}, bf16[64,3,128]{2,0,1:T(8,128)(2,1)S(1)}, u32[]{:S(2)}, u32[]{:S(2)}) collective-permute-start(bf16[64,3,128]{2,0,1:T(8,128)(2,1)S(1)} %get-tuple-element.11), channel_id=1, source_target_pairs={{127,0},{0,1},{1,2},{2,3},{3,4},{4,5},{5,6},{6,7},{7,8},{8,9},{9,1... | collective-permute-start | bytes 147464 | tf_op jit(solution)/shard_map/ppermute | solution.py:13
  231.8 17.7 %collective-permute-start.44 = (bf16[64,3,128]{2,0,1:T(8,128)(2,1)S(1)}, bf16[64,3,128]{2,0,1:T(8,128)(2,1)S(1)}, u32[]{:S(2)}, u32[]{:S(2)}) collective-permute-start(bf16[64,3,128]{2,0,1:T(8,128)(2,1)S(1)} %get-tuple-element.10), channel_id=1, source_target_pairs={{2,0},{3,1},{4,2},{5,3},{6,4},{7,5},{8,6},{9,7},{10,8},{11,9},{12,... | collective-permute-start | bytes 147464 | tf_op jit(solution)/shard_map/ppermute | solution.py:13
  233.8 15.8 %collective-permute-start.45 = (bf16[64,3,128]{2,0,1:T(8,128)(2,1)S(1)}, bf16[64,3,128]{2,0,1:T(8,128)(2,1)S(1)}, u32[]{:S(2)}, u32[]{:S(2)}) collective-permute-start(bf16[64,3,128]{2,0,1:T(8,128)(2,1)S(1)} %get-tuple-element.9), channel_id=1, source_target_pairs={{126,0},{127,1},{0,2},{1,3},{2,4},{3,5},{4,6},{5,7},{6,8},{7,9},{8... | collective-permute-start | bytes 147464 | tf_op jit(solution)/shard_map/ppermute | solution.py:13
  237.7 11.9 %collective-permute-start.46 = (bf16[64,3,128]{2,0,1:T(8,128)(2,1)S(1)}, bf16[64,3,128]{2,0,1:T(8,128)(2,1)S(1)}, u32[]{:S(2)}, u32[]{:S(2)}) collective-permute-start(bf16[64,3,128]{2,0,1:T(8,128)(2,1)S(1)} %get-tuple-element.8), channel_id=1, source_target_pairs={{3,0},{4,1},{5,2},{6,3},{7,4},{8,5},{9,6},{10,7},{11,8},{12,9},{13... | collective-permute-start | bytes 147464 | tf_op jit(solution)/shard_map/ppermute | solution.py:13
  247.6 9.0 %collective-permute-start.47 = (bf16[64,3,128]{2,0,1:T(8,128)(2,1)S(1)}, bf16[64,3,128]{2,0,1:T(8,128)(2,1)S(1)}, u32[]{:S(2)}, u32[]{:S(2)}) collective-permute-start(bf16[64,3,128]{2,0,1:T(8,128)(2,1)S(1)} %get-tuple-element.7), channel_id=1, source_target_pairs={{125,0},{126,1},{127,2},{0,3},{1,4},{2,5},{3,6},{4,7},{5,8},{6,9},... | collective-permute-start | bytes 147464 | tf_op jit(solution)/shard_map/ppermute | solution.py:13
  258.5 13.6 %collective-permute-start.18 = (bf16[64,3,128]{2,1,0:T(4,128)(2,1)S(1)}, bf16[64,3,128]{2,1,0:T(4,128)(2,1)S(1)}, u32[]{:S(2)}, u32[]{:S(2)}) collective-permute-start(bf16[64,3,128]{2,1,0:T(4,128)(2,1)S(1)} %copy.179), channel_id=1, source_target_pairs={{127,0},{0,1},{1,2},{2,3},{3,4},{4,5},{5,6},{6,7},{7,8},{8,9},{9,1... | collective-permute-start | bytes 147464 | tf_op jit(solution)/shard_map/ppermute | solution.py:13
  260.5 19.0 %collective-permute-start.19 = (bf16[64,3,128]{2,1,0:T(4,128)(2,1)S(1)}, bf16[64,3,128]{2,1,0:T(4,128)(2,1)S(1)}, u32[]{:S(2)}, u32[]{:S(2)}) collective-permute-start(bf16[64,3,128]{2,1,0:T(4,128)(2,1)S(1)} %copy.180), channel_id=1, source_target_pairs={{1,0},{2,1},{3,2},{4,3},{5,4},{6,5},{7,6},{8,7},{9,8},{10,9},{11,1... | collective-permute-start | bytes 147464 | tf_op jit(solution)/shard_map/ppermute | solution.py:13
  264.2 15.3 %collective-permute-start.20 = (bf16[64,3,128]{2,1,0:T(4,128)(2,1)S(1)}, bf16[64,3,128]{2,1,0:T(4,128)(2,1)S(1)}, u32[]{:S(2)}, u32[]{:S(2)}) collective-permute-start(bf16[64,3,128]{2,1,0:T(4,128)(2,1)S(1)} %copy.181), channel_id=1, source_target_pairs={{126,0},{127,1},{0,2},{1,3},{2,4},{3,5},{4,6},{5,7},{6,8},{7,9},{8... | collective-permute-start | bytes 147464 | tf_op jit(solution)/shard_map/ppermute | solution.py:13
  266.2 13.3 %collective-permute-start.21 = (bf16[64,3,128]{2,1,0:T(4,128)(2,1)S(1)}, bf16[64,3,128]{2,1,0:T(4,128)(2,1)S(1)}, u32[]{:S(2)}, u32[]{:S(2)}) collective-permute-start(bf16[64,3,128]{2,1,0:T(4,128)(2,1)S(1)} %copy.182), channel_id=1, source_target_pairs={{2,0},{3,1},{4,2},{5,3},{6,4},{7,5},{8,6},{9,7},{10,8},{11,9},{12,... | collective-permute-start | bytes 147464 | tf_op jit(solution)/shard_map/ppermute | solution.py:13
  270.2 9.3 %collective-permute-start.22 = (bf16[64,3,128]{2,1,0:T(4,128)(2,1)S(1)}, bf16[64,3,128]{2,1,0:T(4,128)(2,1)S(1)}, u32[]{:S(2)}, u32[]{:S(2)}) collective-permute-start(bf16[64,3,128]{2,1,0:T(4,128)(2,1)S(1)} %copy.183), channel_id=1, source_target_pairs={{125,0},{126,1},{127,2},{0,3},{1,4},{2,5},{3,6},{4,7},{5,8},{6,9},... | collective-permute-start | bytes 147464 | tf_op jit(solution)/shard_map/ppermute | solution.py:13
  272.1 9.1 %collective-permute-start.23 = (bf16[64,3,128]{2,1,0:T(4,128)(2,1)S(1)}, bf16[64,3,128]{2,1,0:T(4,128)(2,1)S(1)}, u32[]{:S(2)}, u32[]{:S(2)}) collective-permute-start(bf16[64,3,128]{2,1,0:T(4,128)(2,1)S(1)} %copy.184), channel_id=1, source_target_pairs={{3,0},{4,1},{5,2},{6,3},{7,4},{8,5},{9,6},{10,7},{11,8},{12,9},{13... | collective-permute-start | bytes 147464 | tf_op jit(solution)/shard_map/ppermute | solution.py:13
  (16 other events, 276.1 us)
Sparse Core Ops, SparseCore 0:
  258.5 54.5 all-reduce.1
where the time goes:
time: 323 us; the launch traced here: 321 us
  starting transfers between devices  189 us (59%)
  waiting for transfers between devices  51.7 us (16%)
  other arithmetic  31.8 us (10%)
  local copies, waits for them, and re-layouts  25.6 us (8%)
  between operations  15.8 us (5%)
  matrix products  7.16 us (2%)
    ppermute x48, starting transfers between devices, passed_along(): return lax.ppermute(block, axis, route)  189 us
    psum x1, waiting for transfers between devices, shards(): lax.psum(partial_sum.astype(jnp.bfloat16), 'inj').astype(jnp.float32)  29.6 us
    unnamed x4, other arithmetic  28.9 us
    ppermute x48, waiting for transfers between devices, passed_along(): return lax.ppermute(block, axis, route)  22 us
    concatenate x4, local copies, waits for them, and re-layouts, shards(): incoming = jnp.concatenate(send_pieces, axis=1)  7.51 us
  transfers between devices with their start and end apart: 49, of which 5 were waited for; matrix products, arithmetic and copies ran while one was open for 15% of the time, Pallas kernels for 0%

commit v1 on v0

--- a/solution.py
+++ b/solution.py
@@ -93,7 +93,9 @@
             preferred_element_type=jnp.float32,
         )
     partial_sum = accum * (1.0 / set_count)
-    summed = lax.psum(partial_sum.astype(jnp.bfloat16), "inj").astype(jnp.float32)
+    summed = jnp.sum(lax.all_gather(partial_sum.astype(jnp.bfloat16), "inj"), axis=0).astype(
+        jnp.float32
+    )
     portion = block_width // lax.axis_size("inj")
     mine = lax.dynamic_slice_in_dim(summed, lax.axis_index("inj") * portion, portion, 1)
     return (adjoint.reshape(set_count, pore_count), mine.astype(jnp.bfloat16))

time: 323 us -> 299 us (0.926)
  the two profiles are of different devices: /device:TPU:2 before, /device:TPU:1 now
where the time goes in v1:
time: 299 us; the launch traced here: 297 us
  starting transfers between devices  200 us (67%)
  other arithmetic  34.7 us (12%)
  local copies, waits for them, and re-layouts  22.9 us (8%)
  waiting for transfers between devices  16.9 us (6%)
  between operations  15.7 us (5%)
  matrix products  7.11 us (2%)
    ppermute x48, starting transfers between devices, passed_along(): return lax.ppermute(block, axis, route)  200 us
    unnamed x4, other arithmetic  28.9 us
    ppermute x48, waiting for transfers between devices, passed_along(): return lax.ppermute(block, axis, route)  14.1 us
    concatenate x4, local copies, waits for them, and re-layouts, shards(): incoming = jnp.concatenate(send_pieces, axis=1)  7.52 us
  transfers between devices with their start and end apart: 49, of which 6 were waited for; matrix products, arithmetic and copies ran while one was open for 17% of the time, Pallas kernels for 0%

profile of v1, /device:TPU:1, one launch (start us, length us, event | category | flops | bytes accessed | tf_op | source)
XLA Modules:
  0.0 297.4 jit_solution(706017695096365293)
XLA Ops:
  13.3 4.5 %collective-permute-start = (bf16[64,3,128]{2,1,0:T(4,128)(2,1)S(1)}, bf16[64,3,128]{2,1,0:T(4,128)(2,1)S(1)}, u32[]{:S(2)}, u32[]{:S(2)}) collective-permute-start(bf16[64,3,128]{2,1,0:T(4,128)(2,1)S(1)} %copy.197), channel_id=1, source_target_pairs={{127,0},{0,1},{1,2},{2,3},{3,4},{4,5},{5,6},{6,7},{7,8},{8,9},{9,1... | collective-permute-start | bytes 147464 | tf_op jit(solution)/shard_map/ppermute | solution.py:13
  17.8 6.2 %collective-permute-start.1 = (bf16[64,3,128]{2,1,0:T(4,128)(2,1)S(1)}, bf16[64,3,128]{2,1,0:T(4,128)(2,1)S(1)}, u32[]{:S(2)}, u32[]{:S(2)}) collective-permute-start(bf16[64,3,128]{2,1,0:T(4,128)(2,1)S(1)} %copy.198), channel_id=1, source_target_pairs={{1,0},{2,1},{3,2},{4,3},{5,4},{6,5},{7,6},{8,7},{9,8},{10,9},{11,1... | collective-permute-start | bytes 147464 | tf_op jit(solution)/shard_map/ppermute | solution.py:13
  24.1 1.9 collective-permute-start.2
  26.1 7.9 %collective-permute-start.3 = (bf16[64,3,128]{2,1,0:T(4,128)(2,1)S(1)}, bf16[64,3,128]{2,1,0:T(4,128)(2,1)S(1)}, u32[]{:S(2)}, u32[]{:S(2)}) collective-permute-start(bf16[64,3,128]{2,1,0:T(4,128)(2,1)S(1)} %copy.200), channel_id=1, source_target_pairs={{2,0},{3,1},{4,2},{5,3},{6,4},{7,5},{8,6},{9,7},{10,8},{11,9},{12,... | collective-permute-start | bytes 147464 | tf_op jit(solution)/shard_map/ppermute | solution.py:13
  34.1 1.9 collective-permute-start.4
  36.4 28.8 %scatter_custom_fusion.4 = f32[32768]{0:T(1024)S(1)} fusion(s32[4096]{0:T(1024)S(1)} %reshape.171, f32[4096]{0:T(1024)S(1)} %broadcast.101, f32[]{:T(128)} %constant.14.clone.1), kind=kCustom, calls=%fused_computation.80 | custom fusion | flops 4096 | bytes 131076
  66.0 7.0 %collective-permute-start.5 = (bf16[64,3,128]{2,1,0:T(4,128)(2,1)S(1)}, bf16[64,3,128]{2,1,0:T(4,128)(2,1)S(1)}, u32[]{:S(2)}, u32[]{:S(2)}) collective-permute-start(bf16[64,3,128]{2,1,0:T(4,128)(2,1)S(1)} %copy.202), channel_id=1, source_target_pairs={{3,0},{4,1},{5,2},{6,3},{7,4},{8,5},{9,6},{10,7},{11,8},{12,9},{13... | collective-permute-start | bytes 147464 | tf_op jit(solution)/shard_map/ppermute | solution.py:13
  73.1 7.3 %collective-permute-start.24 = (bf16[64,3,128]{2,0,1:T(8,128)(2,1)S(1)}, bf16[64,3,128]{2,0,1:T(8,128)(2,1)S(1)}, u32[]{:S(2)}, u32[]{:S(2)}) collective-permute-start(bf16[64,3,128]{2,0,1:T(8,128)(2,1)S(1)} %get-tuple-element.33), channel_id=1, source_target_pairs={{1,0},{2,1},{3,2},{4,3},{5,4},{6,5},{7,6},{8,7},{9,8},{10,9},{11,1... | collective-permute-start | bytes 147464 | tf_op jit(solution)/shard_map/ppermute | solution.py:13
  80.4 1.9 collective-permute-start.25
  82.3 6.6 %collective-permute-start.26 = (bf16[64,3,128]{2,0,1:T(8,128)(2,1)S(1)}, bf16[64,3,128]{2,0,1:T(8,128)(2,1)S(1)}, u32[]{:S(2)}, u32[]{:S(2)}) collective-permute-start(bf16[64,3,128]{2,0,1:T(8,128)(2,1)S(1)} %get-tuple-element.31), channel_id=1, source_target_pairs={{2,0},{3,1},{4,2},{5,3},{6,4},{7,5},{8,6},{9,7},{10,8},{11,9},{12,... | collective-permute-start | bytes 147464 | tf_op jit(solution)/shard_map/ppermute | solution.py:13
  88.9 1.9 collective-permute-start.27
  90.8 2.8 collective-permute-start.28
  97.3 4.3 %collective-permute-start.29 = (bf16[64,3,128]{2,0,1:T(8,128)(2,1)S(1)}, bf16[64,3,128]{2,0,1:T(8,128)(2,1)S(1)}, u32[]{:S(2)}, u32[]{:S(2)}) collective-permute-start(bf16[64,3,128]{2,0,1:T(8,128)(2,1)S(1)} %get-tuple-element.28), channel_id=1, source_target_pairs={{125,0},{126,1},{127,2},{0,3},{1,4},{2,5},{3,6},{4,7},{5,8},{6,9},... | collective-permute-start | bytes 147464 | tf_op jit(solution)/shard_map/ppermute | solution.py:13
  101.7 4.3 %collective-permute-start.6 = (bf16[64,3,128]{2,1,0:T(4,128)(2,1)S(1)}, bf16[64,3,128]{2,1,0:T(4,128)(2,1)S(1)}, u32[]{:S(2)}, u32[]{:S(2)}) collective-permute-start(bf16[64,3,128]{2,1,0:T(4,128)(2,1)S(1)} %copy.204), channel_id=1, source_target_pairs={{127,0},{0,1},{1,2},{2,3},{3,4},{4,5},{5,6},{6,7},{7,8},{8,9},{9,1... | collective-permute-start | bytes 147464 | tf_op jit(solution)/shard_map/ppermute | solution.py:13
  106.1 1.9 collective-permute-start.7
  108.1 2.0 collective-permute-start.8
  110.2 6.8 %collective-permute-start.9 = (bf16[64,3,128]{2,1,0:T(4,128)(2,1)S(1)}, bf16[64,3,128]{2,1,0:T(4,128)(2,1)S(1)}, u32[]{:S(2)}, u32[]{:S(2)}) collective-permute-start(bf16[64,3,128]{2,1,0:T(4,128)(2,1)S(1)} %copy.207), channel_id=1, source_target_pairs={{2,0},{3,1},{4,2},{5,3},{6,4},{7,5},{8,6},{9,7},{10,8},{11,9},{12,... | collective-permute-start | bytes 147464 | tf_op jit(solution)/shard_map/ppermute | solution.py:13
  117.1 1.9 collective-permute-start.10
  121.4 7.0 %collective-permute-start.11 = (bf16[64,3,128]{2,1,0:T(4,128)(2,1)S(1)}, bf16[64,3,128]{2,1,0:T(4,128)(2,1)S(1)}, u32[]{:S(2)}, u32[]{:S(2)}) collective-permute-start(bf16[64,3,128]{2,1,0:T(4,128)(2,1)S(1)} %copy.209), channel_id=1, source_target_pairs={{3,0},{4,1},{5,2},{6,3},{7,4},{8,5},{9,6},{10,7},{11,8},{12,9},{13... | collective-permute-start | bytes 147464 | tf_op jit(solution)/shard_map/ppermute | solution.py:13
  128.5 7.4 %collective-permute-start.30 = (bf16[64,3,128]{2,0,1:T(8,128)(2,1)S(1)}, bf16[64,3,128]{2,0,1:T(8,128)(2,1)S(1)}, u32[]{:S(2)}, u32[]{:S(2)}) collective-permute-start(bf16[64,3,128]{2,0,1:T(8,128)(2,1)S(1)} %get-tuple-element.26), channel_id=1, source_target_pairs={{1,0},{2,1},{3,2},{4,3},{5,4},{6,5},{7,6},{8,7},{9,8},{10,9},{11,1... | collective-permute-start | bytes 147464 | tf_op jit(solution)/shard_map/ppermute | solution.py:13
  135.9 1.9 collective-permute-start.31
  137.8 6.6 %collective-permute-start.32 = (bf16[64,3,128]{2,0,1:T(8,128)(2,1)S(1)}, bf16[64,3,128]{2,0,1:T(8,128)(2,1)S(1)}, u32[]{:S(2)}, u32[]{:S(2)}) collective-permute-start(bf16[64,3,128]{2,0,1:T(8,128)(2,1)S(1)} %get-tuple-element.24), channel_id=1, source_target_pairs={{2,0},{3,1},{4,2},{5,3},{6,4},{7,5},{8,6},{9,7},{10,8},{11,9},{12,... | collective-permute-start | bytes 147464 | tf_op jit(solution)/shard_map/ppermute | solution.py:13
  144.4 1.9 collective-permute-start.33
  146.4 2.8 collective-permute-start.34
  151.6 4.3 %collective-permute-start.35 = (bf16[64,3,128]{2,0,1:T(8,128)(2,1)S(1)}, bf16[64,3,128]{2,0,1:T(8,128)(2,1)S(1)}, u32[]{:S(2)}, u32[]{:S(2)}) collective-permute-start(bf16[64,3,128]{2,0,1:T(8,128)(2,1)S(1)} %get-tuple-element.21), channel_id=1, source_target_pairs={{125,0},{126,1},{127,2},{0,3},{1,4},{2,5},{3,6},{4,7},{5,8},{6,9},... | collective-permute-start | bytes 147464 | tf_op jit(solution)/shard_map/ppermute | solution.py:13
  156.0 4.6 %collective-permute-done.35 = bf16[64,3,128]{2,0,1:T(8,128)(2,1)S(1)} collective-permute-done((bf16[64,3,128]{2,0,1:T(8,128)(2,1)S(1)}, bf16[64,3,128]{2,0,1:T(8,128)(2,1)S(1)}, u32[]{:S(2)}, u32[]{:S(2)}) %collective-permute-start.35) | collective-permute-done | bytes 49184 | tf_op jit(solution)/shard_map/ppermute | solution.py:13
  163.3 6.7 %collective-permute-start.12 = (bf16[64,3,128]{2,1,0:T(4,128)(2,1)S(1)}, bf16[64,3,128]{2,1,0:T(4,128)(2,1)S(1)}, u32[]{:S(2)}, u32[]{:S(2)}) collective-permute-start(bf16[64,3,128]{2,1,0:T(4,128)(2,1)S(1)} %copy.211), channel_id=1, source_target_pairs={{127,0},{0,1},{1,2},{2,3},{3,4},{4,5},{5,6},{6,7},{7,8},{8,9},{9,1... | collective-permute-start | bytes 147464 | tf_op jit(solution)/shard_map/ppermute | solution.py:13
  172.1 2.0 collective-permute-start.14
  174.2 6.6 %collective-permute-start.15 = (bf16[64,3,128]{2,1,0:T(4,128)(2,1)S(1)}, bf16[64,3,128]{2,1,0:T(4,128)(2,1)}, u32[]{:S(2)}, u32[]{:S(2)}) collective-permute-start(bf16[64,3,128]{2,1,0:T(4,128)(2,1)S(1)} %copy.214), channel_id=1, source_target_pairs={{2,0},{3,1},{4,2},{5,3},{6,4},{7,5},{8,6},{9,7},{10,8},{11,9},{12,... | collective-permute-start | bytes 147464 | tf_op jit(solution)/shard_map/ppermute | solution.py:13
  180.8 1.9 collective-permute-start.16
  184.1 7.0 %collective-permute-start.17 = (bf16[64,3,128]{2,1,0:T(4,128)(2,1)S(1)}, bf16[64,3,128]{2,1,0:T(4,128)(2,1)S(1)}, u32[]{:S(2)}, u32[]{:S(2)}) collective-permute-start(bf16[64,3,128]{2,1,0:T(4,128)(2,1)S(1)} %copy.216), channel_id=1, source_target_pairs={{3,0},{4,1},{5,2},{6,3},{7,4},{8,5},{9,6},{10,7},{11,8},{12,9},{13... | collective-permute-start | bytes 147464 | tf_op jit(solution)/shard_map/ppermute | solution.py:13
  191.1 4.0 %collective-permute-start.36 = (bf16[64,3,128]{2,0,1:T(8,128)(2,1)S(1)}, bf16[64,3,128]{2,0,1:T(8,128)(2,1)S(1)}, u32[]{:S(2)}, u32[]{:S(2)}) collective-permute-start(bf16[64,3,128]{2,0,1:T(8,128)(2,1)S(1)} %get-tuple-element.19), channel_id=1, source_target_pairs={{1,0},{2,1},{3,2},{4,3},{5,4},{6,5},{7,6},{8,7},{9,8},{10,9},{11,1... | collective-permute-start | bytes 147464 | tf_op jit(solution)/shard_map/ppermute | solution.py:13
  197.0 6.6 %collective-permute-start.38 = (bf16[64,3,128]{2,0,1:T(8,128)(2,1)S(1)}, bf16[64,3,128]{2,0,1:T(8,128)(2,1)S(1)}, u32[]{:S(2)}, u32[]{:S(2)}) collective-permute-start(bf16[64,3,128]{2,0,1:T(8,128)(2,1)S(1)} %get-tuple-element.17), channel_id=1, source_target_pairs={{2,0},{3,1},{4,2},{5,3},{6,4},{7,5},{8,6},{9,7},{10,8},{11,9},{12,... | collective-permute-start | bytes 147464 | tf_op jit(solution)/shard_map/ppermute | solution.py:13
  205.6 2.8 collective-permute-start.40
  208.3 3.6 %concatenate.29 = bf16[64,21,128]{2,1,0:T(8,128)(2,1)S(1)} concatenate(bf16[64,3,128]{2,1,0:T(4,128)(2,1)S(1)} %copy.210, bf16[64,3,128]{2,1,0:T(4,128)(2,1)S(1)} %collective-permute-done.12, bf16[64,3,128]{2,1,0:T(4,128)(2,1)S(1)} %collective-permute-done.13, bf16[64,3,128]{2,1,0:T(4,128)(2,1)} %collective-permute-done.14, bf16[64,3,128]{2,1,0:T(4,128)(2,1)} %collective-permute-done.15, ...), dimensions={1} | concatenate | bytes 688128 | tf_op jit(solution)/shard_map/concatenate | solution.py:83
  212.1 4.5 %collective-permute-start.41 = (bf16[64,3,128]{2,0,1:T(8,128)(2,1)S(1)}, bf16[64,3,128]{2,0,1:T(8,128)(2,1)S(1)}, u32[]{:S(2)}, u32[]{:S(2)}) collective-permute-start(bf16[64,3,128]{2,0,1:T(8,128)(2,1)S(1)} %get-tuple-element.14), channel_id=1, source_target_pairs={{125,0},{126,1},{127,2},{0,3},{1,4},{2,5},{3,6},{4,7},{5,8},{6,9},... | collective-permute-start | bytes 147464 | tf_op jit(solution)/shard_map/ppermute | solution.py:13
  217.4 3.8 %collective-permute-done.41 = bf16[64,3,128]{2,0,1:T(8,128)(2,1)S(1)} collective-permute-done((bf16[64,3,128]{2,0,1:T(8,128)(2,1)S(1)}, bf16[64,3,128]{2,0,1:T(8,128)(2,1)S(1)}, u32[]{:S(2)}, u32[]{:S(2)}) %collective-permute-start.41) | collective-permute-done | bytes 49184 | tf_op jit(solution)/shard_map/ppermute | solution.py:13
  223.5 2.8 collective-permute-start.42
  227.1 5.8 %collective-permute-start.43 = (bf16[64,3,128]{2,0,1:T(8,128)(2,1)S(1)}, bf16[64,3,128]{2,0,1:T(8,128)(2,1)S(1)}, u32[]{:S(2)}, u32[]{:S(2)}) collective-permute-start(bf16[64,3,128]{2,0,1:T(8,128)(2,1)S(1)} %get-tuple-element.11), channel_id=1, source_target_pairs={{127,0},{0,1},{1,2},{2,3},{3,4},{4,5},{5,6},{6,7},{7,8},{8,9},{9,1... | collective-permute-start | bytes 147464 | tf_op jit(solution)/shard_map/ppermute | solution.py:13
  232.9 5.5 %collective-permute-start.44 = (bf16[64,3,128]{2,0,1:T(8,128)(2,1)S(1)}, bf16[64,3,128]{2,0,1:T(8,128)(2,1)S(1)}, u32[]{:S(2)}, u32[]{:S(2)}) collective-permute-start(bf16[64,3,128]{2,0,1:T(8,128)(2,1)S(1)} %get-tuple-element.10), channel_id=1, source_target_pairs={{2,0},{3,1},{4,2},{5,3},{6,4},{7,5},{8,6},{9,7},{10,8},{11,9},{12,... | collective-permute-start | bytes 147464 | tf_op jit(solution)/shard_map/ppermute | solution.py:13
  240.4 2.6 collective-permute-start.46
  243.0 4.5 %collective-permute-start.47 = (bf16[64,3,128]{2,0,1:T(8,128)(2,1)S(1)}, bf16[64,3,128]{2,0,1:T(8,128)(2,1)S(1)}, u32[]{:S(2)}, u32[]{:S(2)}) collective-permute-start(bf16[64,3,128]{2,0,1:T(8,128)(2,1)S(1)} %get-tuple-element.7), channel_id=1, source_target_pairs={{125,0},{126,1},{127,2},{0,3},{1,4},{2,5},{3,6},{4,7},{5,8},{6,9},... | collective-permute-start | bytes 147464 | tf_op jit(solution)/shard_map/ppermute | solution.py:13
  247.6 4.4 %collective-permute-done.47 = bf16[64,3,128]{2,0,1:T(8,128)(2,1)S(1)} collective-permute-done((bf16[64,3,128]{2,0,1:T(8,128)(2,1)S(1)}, bf16[64,3,128]{2,0,1:T(8,128)(2,1)S(1)}, u32[]{:S(2)}, u32[]{:S(2)}) %collective-permute-start.47) | collective-permute-done | bytes 49184 | tf_op jit(solution)/shard_map/ppermute | solution.py:13
  255.4 6.9 %collective-permute-start.18 = (bf16[64,3,128]{2,1,0:T(4,128)(2,1)S(1)}, bf16[64,3,128]{2,1,0:T(4,128)(2,1)S(1)}, u32[]{:S(2)}, u32[]{:S(2)}) collective-permute-start(bf16[64,3,128]{2,1,0:T(4,128)(2,1)S(1)} %copy.218), channel_id=1, source_target_pairs={{127,0},{0,1},{1,2},{2,3},{3,4},{4,5},{5,6},{6,7},{7,8},{8,9},{9,1... | collective-permute-start | bytes 147464 | tf_op jit(solution)/shard_map/ppermute | solution.py:13
  264.3 2.0 collective-permute-start.20
  266.4 6.6 %collective-permute-start.21 = (bf16[64,3,128]{2,1,0:T(4,128)(2,1)S(1)}, bf16[64,3,128]{2,1,0:T(4,128)(2,1)S(1)}, u32[]{:S(2)}, u32[]{:S(2)}) collective-permute-start(bf16[64,3,128]{2,1,0:T(4,128)(2,1)S(1)} %copy.221), channel_id=1, source_target_pairs={{2,0},{3,1},{4,2},{5,3},{6,4},{7,5},{8,6},{9,7},{10,8},{11,9},{12,... | collective-permute-start | bytes 147464 | tf_op jit(solution)/shard_map/ppermute | solution.py:13
  275.0 7.0 %collective-permute-start.23 = (bf16[64,3,128]{2,1,0:T(4,128)(2,1)S(1)}, bf16[64,3,128]{2,1,0:T(4,128)(2,1)S(1)}, u32[]{:S(2)}, u32[]{:S(2)}) collective-permute-start(bf16[64,3,128]{2,1,0:T(4,128)(2,1)S(1)} %copy.223), channel_id=1, source_target_pairs={{3,0},{4,1},{5,2},{6,3},{7,4},{8,5},{9,6},{10,7},{11,8},{12,9},{13... | collective-permute-start | bytes 147464 | tf_op jit(solution)/shard_map/ppermute | solution.py:13
  285.5 2.8 all-gather.3.cloned.1.call-done
  (201 shorter events, 45.3 us)
Async XLA Ops:
  7.2 281.0 %all-gather.3.cloned.1.call-start = ((), (), s32[]{:S(2)}) async-start(), calls=%async_computation | async-start | bytes 1966080 | tf_op jit(solution)/shard_map/all_gather | solution.py:96
  13.3 52.8 %collective-permute-start = (bf16[64,3,128]{2,1,0:T(4,128)(2,1)S(1)}, bf16[64,3,128]{2,1,0:T(4,128)(2,1)S(1)}, u32[]{:S(2)}, u32[]{:S(2)}) collective-permute-start(bf16[64,3,128]{2,1,0:T(4,128)(2,1)S(1)} %copy.197), channel_id=1, source_target_pairs={{127,0},{0,1},{1,2},{2,3},{3,4},{4,5},{5,6},{6,7},{7,8},{8,9},{9,1... | collective-permute-start | bytes 147464 | tf_op jit(solution)/shard_map/ppermute | solution.py:13
  17.8 55.2 %collective-permute-start.1 = (bf16[64,3,128]{2,1,0:T(4,128)(2,1)S(1)}, bf16[64,3,128]{2,1,0:T(4,128)(2,1)S(1)}, u32[]{:S(2)}, u32[]{:S(2)}) collective-permute-start(bf16[64,3,128]{2,1,0:T(4,128)(2,1)S(1)} %copy.198), channel_id=1, source_target_pairs={{1,0},{2,1},{3,2},{4,3},{5,4},{6,5},{7,6},{8,7},{9,8},{10,9},{11,1... | collective-permute-start | bytes 147464 | tf_op jit(solution)/shard_map/ppermute | solution.py:13
  24.1 56.3 %collective-permute-start.2 = (bf16[64,3,128]{2,1,0:T(4,128)(2,1)S(1)}, bf16[64,3,128]{2,1,0:T(4,128)(2,1)S(1)}, u32[]{:S(2)}, u32[]{:S(2)}) collective-permute-start(bf16[64,3,128]{2,1,0:T(4,128)(2,1)S(1)} %copy.199), channel_id=1, source_target_pairs={{126,0},{127,1},{0,2},{1,3},{2,4},{3,5},{4,6},{5,7},{6,8},{7,9},{8... | collective-permute-start | bytes 147464 | tf_op jit(solution)/shard_map/ppermute | solution.py:13
  26.1 56.2 %collective-permute-start.3 = (bf16[64,3,128]{2,1,0:T(4,128)(2,1)S(1)}, bf16[64,3,128]{2,1,0:T(4,128)(2,1)S(1)}, u32[]{:S(2)}, u32[]{:S(2)}) collective-permute-start(bf16[64,3,128]{2,1,0:T(4,128)(2,1)S(1)} %copy.200), channel_id=1, source_target_pairs={{2,0},{3,1},{4,2},{5,3},{6,4},{7,5},{8,6},{9,7},{10,8},{11,9},{12,... | collective-permute-start | bytes 147464 | tf_op jit(solution)/shard_map/ppermute | solution.py:13
  34.1 54.8 %collective-permute-start.4 = (bf16[64,3,128]{2,1,0:T(4,128)(2,1)S(1)}, bf16[64,3,128]{2,1,0:T(4,128)(2,1)S(1)}, u32[]{:S(2)}, u32[]{:S(2)}) collective-permute-start(bf16[64,3,128]{2,1,0:T(4,128)(2,1)S(1)} %copy.201), channel_id=1, source_target_pairs={{125,0},{126,1},{127,2},{0,3},{1,4},{2,5},{3,6},{4,7},{5,8},{6,9},... | collective-permute-start | bytes 147464 | tf_op jit(solution)/shard_map/ppermute | solution.py:13
  66.0 24.8 %collective-permute-start.5 = (bf16[64,3,128]{2,1,0:T(4,128)(2,1)S(1)}, bf16[64,3,128]{2,1,0:T(4,128)(2,1)S(1)}, u32[]{:S(2)}, u32[]{:S(2)}) collective-permute-start(bf16[64,3,128]{2,1,0:T(4,128)(2,1)S(1)} %copy.202), channel_id=1, source_target_pairs={{3,0},{4,1},{5,2},{6,3},{7,4},{8,5},{9,6},{10,7},{11,8},{12,9},{13... | collective-permute-start | bytes 147464 | tf_op jit(solution)/shard_map/ppermute | solution.py:13
  73.1 24.2 %collective-permute-start.24 = (bf16[64,3,128]{2,0,1:T(8,128)(2,1)S(1)}, bf16[64,3,128]{2,0,1:T(8,128)(2,1)S(1)}, u32[]{:S(2)}, u32[]{:S(2)}) collective-permute-start(bf16[64,3,128]{2,0,1:T(8,128)(2,1)S(1)} %get-tuple-element.33), channel_id=1, source_target_pairs={{1,0},{2,1},{3,2},{4,3},{5,4},{6,5},{7,6},{8,7},{9,8},{10,9},{11,1... | collective-permute-start | bytes 147464 | tf_op jit(solution)/shard_map/ppermute | solution.py:13
  80.4 21.3 %collective-permute-start.25 = (bf16[64,3,128]{2,0,1:T(8,128)(2,1)S(1)}, bf16[64,3,128]{2,0,1:T(8,128)(2,1)S(1)}, u32[]{:S(2)}, u32[]{:S(2)}) collective-permute-start(bf16[64,3,128]{2,0,1:T(8,128)(2,1)S(1)} %get-tuple-element.32), channel_id=1, source_target_pairs={{127,0},{0,1},{1,2},{2,3},{3,4},{4,5},{5,6},{6,7},{7,8},{8,9},{9,1... | collective-permute-start | bytes 147464 | tf_op jit(solution)/shard_map/ppermute | solution.py:13
  82.3 23.8 %collective-permute-start.26 = (bf16[64,3,128]{2,0,1:T(8,128)(2,1)S(1)}, bf16[64,3,128]{2,0,1:T(8,128)(2,1)S(1)}, u32[]{:S(2)}, u32[]{:S(2)}) collective-permute-start(bf16[64,3,128]{2,0,1:T(8,128)(2,1)S(1)} %get-tuple-element.31), channel_id=1, source_target_pairs={{2,0},{3,1},{4,2},{5,3},{6,4},{7,5},{8,6},{9,7},{10,8},{11,9},{12,... | collective-permute-start | bytes 147464 | tf_op jit(solution)/shard_map/ppermute | solution.py:13
  88.9 19.2 %collective-permute-start.27 = (bf16[64,3,128]{2,0,1:T(8,128)(2,1)S(1)}, bf16[64,3,128]{2,0,1:T(8,128)(2,1)S(1)}, u32[]{:S(2)}, u32[]{:S(2)}) collective-permute-start(bf16[64,3,128]{2,0,1:T(8,128)(2,1)S(1)} %get-tuple-element.30), channel_id=1, source_target_pairs={{126,0},{127,1},{0,2},{1,3},{2,4},{3,5},{4,6},{5,7},{6,8},{7,9},{8... | collective-permute-start | bytes 147464 | tf_op jit(solution)/shard_map/ppermute | solution.py:13
  90.8 19.4 %collective-permute-start.28 = (bf16[64,3,128]{2,0,1:T(8,128)(2,1)S(1)}, bf16[64,3,128]{2,0,1:T(8,128)(2,1)S(1)}, u32[]{:S(2)}, u32[]{:S(2)}) collective-permute-start(bf16[64,3,128]{2,0,1:T(8,128)(2,1)S(1)} %get-tuple-element.29), channel_id=1, source_target_pairs={{3,0},{4,1},{5,2},{6,3},{7,4},{8,5},{9,6},{10,7},{11,8},{12,9},{13... | collective-permute-start | bytes 147464 | tf_op jit(solution)/shard_map/ppermute | solution.py:13
  97.3 19.8 %collective-permute-start.29 = (bf16[64,3,128]{2,0,1:T(8,128)(2,1)S(1)}, bf16[64,3,128]{2,0,1:T(8,128)(2,1)S(1)}, u32[]{:S(2)}, u32[]{:S(2)}) collective-permute-start(bf16[64,3,128]{2,0,1:T(8,128)(2,1)S(1)} %get-tuple-element.28), channel_id=1, source_target_pairs={{125,0},{126,1},{127,2},{0,3},{1,4},{2,5},{3,6},{4,7},{5,8},{6,9},... | collective-permute-start | bytes 147464 | tf_op jit(solution)/shard_map/ppermute | solution.py:13
  101.7 19.7 %collective-permute-start.6 = (bf16[64,3,128]{2,1,0:T(4,128)(2,1)S(1)}, bf16[64,3,128]{2,1,0:T(4,128)(2,1)S(1)}, u32[]{:S(2)}, u32[]{:S(2)}) collective-permute-start(bf16[64,3,128]{2,1,0:T(4,128)(2,1)S(1)} %copy.204), channel_id=1, source_target_pairs={{127,0},{0,1},{1,2},{2,3},{3,4},{4,5},{5,6},{6,7},{7,8},{8,9},{9,1... | collective-permute-start | bytes 147464 | tf_op jit(solution)/shard_map/ppermute | solution.py:13
  106.1 22.4 %collective-permute-start.7 = (bf16[64,3,128]{2,1,0:T(4,128)(2,1)S(1)}, bf16[64,3,128]{2,1,0:T(4,128)(2,1)S(1)}, u32[]{:S(2)}, u32[]{:S(2)}) collective-permute-start(bf16[64,3,128]{2,1,0:T(4,128)(2,1)S(1)} %copy.205), channel_id=1, source_target_pairs={{1,0},{2,1},{3,2},{4,3},{5,4},{6,5},{7,6},{8,7},{9,8},{10,9},{11,1... | collective-permute-start | bytes 147464 | tf_op jit(solution)/shard_map/ppermute | solution.py:13
  108.1 27.8 %collective-permute-start.8 = (bf16[64,3,128]{2,1,0:T(4,128)(2,1)S(1)}, bf16[64,3,128]{2,1,0:T(4,128)(2,1)S(1)}, u32[]{:S(2)}, u32[]{:S(2)}) collective-permute-start(bf16[64,3,128]{2,1,0:T(4,128)(2,1)S(1)} %copy.206), channel_id=1, source_target_pairs={{126,0},{127,1},{0,2},{1,3},{2,4},{3,5},{4,6},{5,7},{6,8},{7,9},{8... | collective-permute-start | bytes 147464 | tf_op jit(solution)/shard_map/ppermute | solution.py:13
  110.2 27.6 %collective-permute-start.9 = (bf16[64,3,128]{2,1,0:T(4,128)(2,1)S(1)}, bf16[64,3,128]{2,1,0:T(4,128)(2,1)S(1)}, u32[]{:S(2)}, u32[]{:S(2)}) collective-permute-start(bf16[64,3,128]{2,1,0:T(4,128)(2,1)S(1)} %copy.207), channel_id=1, source_target_pairs={{2,0},{3,1},{4,2},{5,3},{6,4},{7,5},{8,6},{9,7},{10,8},{11,9},{12,... | collective-permute-start | bytes 147464 | tf_op jit(solution)/shard_map/ppermute | solution.py:13
  117.1 27.3 %collective-permute-start.10 = (bf16[64,3,128]{2,1,0:T(4,128)(2,1)S(1)}, bf16[64,3,128]{2,1,0:T(4,128)(2,1)S(1)}, u32[]{:S(2)}, u32[]{:S(2)}) collective-permute-start(bf16[64,3,128]{2,1,0:T(4,128)(2,1)S(1)} %copy.208), channel_id=1, source_target_pairs={{125,0},{126,1},{127,2},{0,3},{1,4},{2,5},{3,6},{4,7},{5,8},{6,9},... | collective-permute-start | bytes 147464 | tf_op jit(solution)/shard_map/ppermute | solution.py:13
  121.4 25.0 %collective-permute-start.11 = (bf16[64,3,128]{2,1,0:T(4,128)(2,1)S(1)}, bf16[64,3,128]{2,1,0:T(4,128)(2,1)S(1)}, u32[]{:S(2)}, u32[]{:S(2)}) collective-permute-start(bf16[64,3,128]{2,1,0:T(4,128)(2,1)S(1)} %copy.209), channel_id=1, source_target_pairs={{3,0},{4,1},{5,2},{6,3},{7,4},{8,5},{9,6},{10,7},{11,8},{12,9},{13... | collective-permute-start | bytes 147464 | tf_op jit(solution)/shard_map/ppermute | solution.py:13
  128.5 23.1 %collective-permute-start.30 = (bf16[64,3,128]{2,0,1:T(8,128)(2,1)S(1)}, bf16[64,3,128]{2,0,1:T(8,128)(2,1)S(1)}, u32[]{:S(2)}, u32[]{:S(2)}) collective-permute-start(bf16[64,3,128]{2,0,1:T(8,128)(2,1)S(1)} %get-tuple-element.26), channel_id=1, source_target_pairs={{1,0},{2,1},{3,2},{4,3},{5,4},{6,5},{7,6},{8,7},{9,8},{10,9},{11,1... | collective-permute-start | bytes 147464 | tf_op jit(solution)/shard_map/ppermute | solution.py:13
  135.9 20.0 %collective-permute-start.31 = (bf16[64,3,128]{2,0,1:T(8,128)(2,1)S(1)}, bf16[64,3,128]{2,0,1:T(8,128)(2,1)S(1)}, u32[]{:S(2)}, u32[]{:S(2)}) collective-permute-start(bf16[64,3,128]{2,0,1:T(8,128)(2,1)S(1)} %get-tuple-element.25), channel_id=1, source_target_pairs={{127,0},{0,1},{1,2},{2,3},{3,4},{4,5},{5,6},{6,7},{7,8},{8,9},{9,1... | collective-permute-start | bytes 147464 | tf_op jit(solution)/shard_map/ppermute | solution.py:13
  137.8 18.1 %collective-permute-start.32 = (bf16[64,3,128]{2,0,1:T(8,128)(2,1)S(1)}, bf16[64,3,128]{2,0,1:T(8,128)(2,1)S(1)}, u32[]{:S(2)}, u32[]{:S(2)}) collective-permute-start(bf16[64,3,128]{2,0,1:T(8,128)(2,1)S(1)} %get-tuple-element.24), channel_id=1, source_target_pairs={{2,0},{3,1},{4,2},{5,3},{6,4},{7,5},{8,6},{9,7},{10,8},{11,9},{12,... | collective-permute-start | bytes 147464 | tf_op jit(solution)/shard_map/ppermute | solution.py:13
  144.4 11.5 %collective-permute-start.33 = (bf16[64,3,128]{2,0,1:T(8,128)(2,1)S(1)}, bf16[64,3,128]{2,0,1:T(8,128)(2,1)S(1)}, u32[]{:S(2)}, u32[]{:S(2)}) collective-permute-start(bf16[64,3,128]{2,0,1:T(8,128)(2,1)S(1)} %get-tuple-element.23), channel_id=1, source_target_pairs={{126,0},{127,1},{0,2},{1,3},{2,4},{3,5},{4,6},{5,7},{6,8},{7,9},{8... | collective-permute-start | bytes 147464 | tf_op jit(solution)/shard_map/ppermute | solution.py:13
  146.4 9.6 %collective-permute-start.34 = (bf16[64,3,128]{2,0,1:T(8,128)(2,1)S(1)}, bf16[64,3,128]{2,0,1:T(8,128)(2,1)S(1)}, u32[]{:S(2)}, u32[]{:S(2)}) collective-permute-start(bf16[64,3,128]{2,0,1:T(8,128)(2,1)S(1)} %get-tuple-element.22), channel_id=1, source_target_pairs={{3,0},{4,1},{5,2},{6,3},{7,4},{8,5},{9,6},{10,7},{11,8},{12,9},{13... | collective-permute-start | bytes 147464 | tf_op jit(solution)/shard_map/ppermute | solution.py:13
  151.6 9.0 %collective-permute-start.35 = (bf16[64,3,128]{2,0,1:T(8,128)(2,1)S(1)}, bf16[64,3,128]{2,0,1:T(8,128)(2,1)S(1)}, u32[]{:S(2)}, u32[]{:S(2)}) collective-permute-start(bf16[64,3,128]{2,0,1:T(8,128)(2,1)S(1)} %get-tuple-element.21), channel_id=1, source_target_pairs={{125,0},{126,1},{127,2},{0,3},{1,4},{2,5},{3,6},{4,7},{5,8},{6,9},... | collective-permute-start | bytes 147464 | tf_op jit(solution)/shard_map/ppermute | solution.py:13
  163.3 20.7 %collective-permute-start.12 = (bf16[64,3,128]{2,1,0:T(4,128)(2,1)S(1)}, bf16[64,3,128]{2,1,0:T(4,128)(2,1)S(1)}, u32[]{:S(2)}, u32[]{:S(2)}) collective-permute-start(bf16[64,3,128]{2,1,0:T(4,128)(2,1)S(1)} %copy.211), channel_id=1, source_target_pairs={{127,0},{0,1},{1,2},{2,3},{3,4},{4,5},{5,6},{6,7},{7,8},{8,9},{9,1... | collective-permute-start | bytes 147464 | tf_op jit(solution)/shard_map/ppermute | solution.py:13
  170.1 21.0 %collective-permute-start.13 = (bf16[64,3,128]{2,1,0:T(4,128)(2,1)S(1)}, bf16[64,3,128]{2,1,0:T(4,128)(2,1)S(1)}, u32[]{:S(2)}, u32[]{:S(2)}) collective-permute-start(bf16[64,3,128]{2,1,0:T(4,128)(2,1)S(1)} %copy.212), channel_id=1, source_target_pairs={{1,0},{2,1},{3,2},{4,3},{5,4},{6,5},{7,6},{8,7},{9,8},{10,9},{11,1... | collective-permute-start | bytes 147464 | tf_op jit(solution)/shard_map/ppermute | solution.py:13
  172.1 23.0 %collective-permute-start.14 = (bf16[64,3,128]{2,1,0:T(4,128)(2,1)S(1)}, bf16[64,3,128]{2,1,0:T(4,128)(2,1)}, u32[]{:S(2)}, u32[]{:S(2)}) collective-permute-start(bf16[64,3,128]{2,1,0:T(4,128)(2,1)S(1)} %copy.213), channel_id=1, source_target_pairs={{126,0},{127,1},{0,2},{1,3},{2,4},{3,5},{4,6},{5,7},{6,8},{7,9},{8... | collective-permute-start | bytes 147464 | tf_op jit(solution)/shard_map/ppermute | solution.py:13
  174.2 22.9 %collective-permute-start.15 = (bf16[64,3,128]{2,1,0:T(4,128)(2,1)S(1)}, bf16[64,3,128]{2,1,0:T(4,128)(2,1)}, u32[]{:S(2)}, u32[]{:S(2)}) collective-permute-start(bf16[64,3,128]{2,1,0:T(4,128)(2,1)S(1)} %copy.214), channel_id=1, source_target_pairs={{2,0},{3,1},{4,2},{5,3},{6,4},{7,5},{8,6},{9,7},{10,8},{11,9},{12,... | collective-permute-start | bytes 147464 | tf_op jit(solution)/shard_map/ppermute | solution.py:13
  180.8 22.8 %collective-permute-start.16 = (bf16[64,3,128]{2,1,0:T(4,128)(2,1)S(1)}, bf16[64,3,128]{2,1,0:T(4,128)(2,1)}, u32[]{:S(2)}, u32[]{:S(2)}) collective-permute-start(bf16[64,3,128]{2,1,0:T(4,128)(2,1)S(1)} %copy.215), channel_id=1, source_target_pairs={{125,0},{126,1},{127,2},{0,3},{1,4},{2,5},{3,6},{4,7},{5,8},{6,9},... | collective-permute-start | bytes 147464 | tf_op jit(solution)/shard_map/ppermute | solution.py:13
  184.1 21.5 %collective-permute-start.17 = (bf16[64,3,128]{2,1,0:T(4,128)(2,1)S(1)}, bf16[64,3,128]{2,1,0:T(4,128)(2,1)S(1)}, u32[]{:S(2)}, u32[]{:S(2)}) collective-permute-start(bf16[64,3,128]{2,1,0:T(4,128)(2,1)S(1)} %copy.216), channel_id=1, source_target_pairs={{3,0},{4,1},{5,2},{6,3},{7,4},{8,5},{9,6},{10,7},{11,8},{12,9},{13... | collective-permute-start | bytes 147464 | tf_op jit(solution)/shard_map/ppermute | solution.py:13
  191.1 21.0 %collective-permute-start.36 = (bf16[64,3,128]{2,0,1:T(8,128)(2,1)S(1)}, bf16[64,3,128]{2,0,1:T(8,128)(2,1)S(1)}, u32[]{:S(2)}, u32[]{:S(2)}) collective-permute-start(bf16[64,3,128]{2,0,1:T(8,128)(2,1)S(1)} %get-tuple-element.19), channel_id=1, source_target_pairs={{1,0},{2,1},{3,2},{4,3},{5,4},{6,5},{7,6},{8,7},{9,8},{10,9},{11,1... | collective-permute-start | bytes 147464 | tf_op jit(solution)/shard_map/ppermute | solution.py:13
  195.1 21.5 %collective-permute-start.37 = (bf16[64,3,128]{2,0,1:T(8,128)(2,1)S(1)}, bf16[64,3,128]{2,0,1:T(8,128)(2,1)S(1)}, u32[]{:S(2)}, u32[]{:S(2)}) collective-permute-start(bf16[64,3,128]{2,0,1:T(8,128)(2,1)S(1)} %get-tuple-element.18), channel_id=1, source_target_pairs={{127,0},{0,1},{1,2},{2,3},{3,4},{4,5},{5,6},{6,7},{7,8},{8,9},{9,1... | collective-permute-start | bytes 147464 | tf_op jit(solution)/shard_map/ppermute | solution.py:13
  197.0 19.6 %collective-permute-start.38 = (bf16[64,3,128]{2,0,1:T(8,128)(2,1)S(1)}, bf16[64,3,128]{2,0,1:T(8,128)(2,1)S(1)}, u32[]{:S(2)}, u32[]{:S(2)}) collective-permute-start(bf16[64,3,128]{2,0,1:T(8,128)(2,1)S(1)} %get-tuple-element.17), channel_id=1, source_target_pairs={{2,0},{3,1},{4,2},{5,3},{6,4},{7,5},{8,6},{9,7},{10,8},{11,9},{12,... | collective-permute-start | bytes 147464 | tf_op jit(solution)/shard_map/ppermute | solution.py:13
  203.6 13.1 %collective-permute-start.39 = (bf16[64,3,128]{2,0,1:T(8,128)(2,1)S(1)}, bf16[64,3,128]{2,0,1:T(8,128)(2,1)S(1)}, u32[]{:S(2)}, u32[]{:S(2)}) collective-permute-start(bf16[64,3,128]{2,0,1:T(8,128)(2,1)S(1)} %get-tuple-element.16), channel_id=1, source_target_pairs={{126,0},{127,1},{0,2},{1,3},{2,4},{3,5},{4,6},{5,7},{6,8},{7,9},{8... | collective-permute-start | bytes 147464 | tf_op jit(solution)/shard_map/ppermute | solution.py:13
  205.6 11.1 %collective-permute-start.40 = (bf16[64,3,128]{2,0,1:T(8,128)(2,1)S(1)}, bf16[64,3,128]{2,0,1:T(8,128)(2,1)S(1)}, u32[]{:S(2)}, u32[]{:S(2)}) collective-permute-start(bf16[64,3,128]{2,0,1:T(8,128)(2,1)S(1)} %get-tuple-element.15), channel_id=1, source_target_pairs={{3,0},{4,1},{5,2},{6,3},{7,4},{8,5},{9,6},{10,7},{11,8},{12,9},{13... | collective-permute-start | bytes 147464 | tf_op jit(solution)/shard_map/ppermute | solution.py:13
  212.1 9.0 %collective-permute-start.41 = (bf16[64,3,128]{2,0,1:T(8,128)(2,1)S(1)}, bf16[64,3,128]{2,0,1:T(8,128)(2,1)S(1)}, u32[]{:S(2)}, u32[]{:S(2)}) collective-permute-start(bf16[64,3,128]{2,0,1:T(8,128)(2,1)S(1)} %get-tuple-element.14), channel_id=1, source_target_pairs={{125,0},{126,1},{127,2},{0,3},{1,4},{2,5},{3,6},{4,7},{5,8},{6,9},... | collective-permute-start | bytes 147464 | tf_op jit(solution)/shard_map/ppermute | solution.py:13
  223.5 19.5 %collective-permute-start.42 = (bf16[64,3,128]{2,0,1:T(8,128)(2,1)S(1)}, bf16[64,3,128]{2,0,1:T(8,128)(2,1)S(1)}, u32[]{:S(2)}, u32[]{:S(2)}) collective-permute-start(bf16[64,3,128]{2,0,1:T(8,128)(2,1)S(1)} %get-tuple-element.12), channel_id=1, source_target_pairs={{1,0},{2,1},{3,2},{4,3},{5,4},{6,5},{7,6},{8,7},{9,8},{10,9},{11,1... | collective-permute-start | bytes 147464 | tf_op jit(solution)/shard_map/ppermute | solution.py:13
  227.1 20.4 %collective-permute-start.43 = (bf16[64,3,128]{2,0,1:T(8,128)(2,1)S(1)}, bf16[64,3,128]{2,0,1:T(8,128)(2,1)S(1)}, u32[]{:S(2)}, u32[]{:S(2)}) collective-permute-start(bf16[64,3,128]{2,0,1:T(8,128)(2,1)S(1)} %get-tuple-element.11), channel_id=1, source_target_pairs={{127,0},{0,1},{1,2},{2,3},{3,4},{4,5},{5,6},{6,7},{7,8},{8,9},{9,1... | collective-permute-start | bytes 147464 | tf_op jit(solution)/shard_map/ppermute | solution.py:13
  232.9 14.6 %collective-permute-start.44 = (bf16[64,3,128]{2,0,1:T(8,128)(2,1)S(1)}, bf16[64,3,128]{2,0,1:T(8,128)(2,1)S(1)}, u32[]{:S(2)}, u32[]{:S(2)}) collective-permute-start(bf16[64,3,128]{2,0,1:T(8,128)(2,1)S(1)} %get-tuple-element.10), channel_id=1, source_target_pairs={{2,0},{3,1},{4,2},{5,3},{6,4},{7,5},{8,6},{9,7},{10,8},{11,9},{12,... | collective-permute-start | bytes 147464 | tf_op jit(solution)/shard_map/ppermute | solution.py:13
  238.5 9.1 %collective-permute-start.45 = (bf16[64,3,128]{2,0,1:T(8,128)(2,1)S(1)}, bf16[64,3,128]{2,0,1:T(8,128)(2,1)S(1)}, u32[]{:S(2)}, u32[]{:S(2)}) collective-permute-start(bf16[64,3,128]{2,0,1:T(8,128)(2,1)S(1)} %get-tuple-element.9), channel_id=1, source_target_pairs={{126,0},{127,1},{0,2},{1,3},{2,4},{3,5},{4,6},{5,7},{6,8},{7,9},{8... | collective-permute-start | bytes 147464 | tf_op jit(solution)/shard_map/ppermute | solution.py:13
  243.0 9.0 %collective-permute-start.47 = (bf16[64,3,128]{2,0,1:T(8,128)(2,1)S(1)}, bf16[64,3,128]{2,0,1:T(8,128)(2,1)S(1)}, u32[]{:S(2)}, u32[]{:S(2)}) collective-permute-start(bf16[64,3,128]{2,0,1:T(8,128)(2,1)S(1)} %get-tuple-element.7), channel_id=1, source_target_pairs={{125,0},{126,1},{127,2},{0,3},{1,4},{2,5},{3,6},{4,7},{5,8},{6,9},... | collective-permute-start | bytes 147464 | tf_op jit(solution)/shard_map/ppermute | solution.py:13
  255.4 19.6 %collective-permute-start.18 = (bf16[64,3,128]{2,1,0:T(4,128)(2,1)S(1)}, bf16[64,3,128]{2,1,0:T(4,128)(2,1)S(1)}, u32[]{:S(2)}, u32[]{:S(2)}) collective-permute-start(bf16[64,3,128]{2,1,0:T(4,128)(2,1)S(1)} %copy.218), channel_id=1, source_target_pairs={{127,0},{0,1},{1,2},{2,3},{3,4},{4,5},{5,6},{6,7},{7,8},{8,9},{9,1... | collective-permute-start | bytes 147464 | tf_op jit(solution)/shard_map/ppermute | solution.py:13
  262.3 19.7 %collective-permute-start.19 = (bf16[64,3,128]{2,1,0:T(4,128)(2,1)S(1)}, bf16[64,3,128]{2,1,0:T(4,128)(2,1)S(1)}, u32[]{:S(2)}, u32[]{:S(2)}) collective-permute-start(bf16[64,3,128]{2,1,0:T(4,128)(2,1)S(1)} %copy.219), channel_id=1, source_target_pairs={{1,0},{2,1},{3,2},{4,3},{5,4},{6,5},{7,6},{8,7},{9,8},{10,9},{11,1... | collective-permute-start | bytes 147464 | tf_op jit(solution)/shard_map/ppermute | solution.py:13
  264.3 17.8 %collective-permute-start.20 = (bf16[64,3,128]{2,1,0:T(4,128)(2,1)S(1)}, bf16[64,3,128]{2,1,0:T(4,128)(2,1)S(1)}, u32[]{:S(2)}, u32[]{:S(2)}) collective-permute-start(bf16[64,3,128]{2,1,0:T(4,128)(2,1)S(1)} %copy.220), channel_id=1, source_target_pairs={{126,0},{127,1},{0,2},{1,3},{2,4},{3,5},{4,6},{5,7},{6,8},{7,9},{8... | collective-permute-start | bytes 147464 | tf_op jit(solution)/shard_map/ppermute | solution.py:13
  266.4 15.7 %collective-permute-start.21 = (bf16[64,3,128]{2,1,0:T(4,128)(2,1)S(1)}, bf16[64,3,128]{2,1,0:T(4,128)(2,1)S(1)}, u32[]{:S(2)}, u32[]{:S(2)}) collective-permute-start(bf16[64,3,128]{2,1,0:T(4,128)(2,1)S(1)} %copy.221), channel_id=1, source_target_pairs={{2,0},{3,1},{4,2},{5,3},{6,4},{7,5},{8,6},{9,7},{10,8},{11,9},{12,... | collective-permute-start | bytes 147464 | tf_op jit(solution)/shard_map/ppermute | solution.py:13
  273.0 9.4 %collective-permute-start.22 = (bf16[64,3,128]{2,1,0:T(4,128)(2,1)S(1)}, bf16[64,3,128]{2,1,0:T(4,128)(2,1)S(1)}, u32[]{:S(2)}, u32[]{:S(2)}) collective-permute-start(bf16[64,3,128]{2,1,0:T(4,128)(2,1)S(1)} %copy.222), channel_id=1, source_target_pairs={{125,0},{126,1},{127,2},{0,3},{1,4},{2,5},{3,6},{4,7},{5,8},{6,9},... | collective-permute-start | bytes 147464 | tf_op jit(solution)/shard_map/ppermute | solution.py:13
  275.0 8.3 %collective-permute-start.23 = (bf16[64,3,128]{2,1,0:T(4,128)(2,1)S(1)}, bf16[64,3,128]{2,1,0:T(4,128)(2,1)S(1)}, u32[]{:S(2)}, u32[]{:S(2)}) collective-permute-start(bf16[64,3,128]{2,1,0:T(4,128)(2,1)S(1)} %copy.223), channel_id=1, source_target_pairs={{3,0},{4,1},{5,2},{6,3},{7,4},{8,5},{9,6},{10,7},{11,8},{12,9},{13... | collective-permute-start | bytes 147464 | tf_op jit(solution)/shard_map/ppermute | solution.py:13
  (8 other events, 164.2 us)
Sparse Core Ops, SparseCore 0:
  253.9 34.2 all-gather.2
